TPU v7x, 256 devices: a whole 4x4x8 slice. The times are simulated.
256 devices in a mesh: gx: 16 (over z_lo, x), gy: 4 (over z_hi, core), gz: 4 (over y).
Axes of the slice: x: 4, y: 4, z: 8 (z_hi: 2, z_lo: 4; z = z_hi * 4 + z_lo), core: 2. Of those that a mesh axis runs over, the one named last changes fastest.
Arguments:
- order_parameter: float32 [64, 512, 512], P('gx', 'gy', 'gz'), may hold values from -1 to 1
- dissolved_species: float32 [64, 512, 512], P('gx', 'gy', 'gz'), may hold values from -0.8 to 0.2
- broad_undercool: float32 [128, 128, 16], P('gy', 'gz'), may hold values from -2.4 to 2.4
Outputs:
- phase_out: float32 [64, 512, 512], P('gx', 'gy', 'gz')
- solute_out: float32 [64, 512, 512], P('gx', 'gy', 'gz')
- temperature_out: float32 [128, 128, 16], P('gy', 'gz')
All inputs are finite; a program needn't handle non-finite values.
Results may differ from a plain program's by a relative error of at most 0.0001.
Values sent between devices are 32-bit elements; how exact they have to be, the bound alone decides.
A program may use at most 64 MiB of HBM per device.

v0:
```python
import jax
import jax.numpy as jnp
from jax import lax
from jax.sharding import PartitionSpec as P

FACTOR = 4
SUBSTEPS = 4


TIME_INCREMENT = 0.1
COUPLING = 3.0
PARTITION = 0.3
DIFFUSION = 1.0
THERMAL_SPREAD = 1.2
FREEZING_WARMTH = 2.0


def padded_2(cells, sides, width):
    for axis, dim in sides:
        count = lax.axis_size(axis)
        head = lax.slice_in_dim(cells, 0, width, axis=dim)
        tail = lax.slice_in_dim(cells, cells.shape[dim] - width, cells.shape[dim], axis=dim)
        cells = jnp.concatenate(
            [
                lax.ppermute(tail, axis, [(i, (i + 1) % count) for i in range(count)]),
                cells,
                lax.ppermute(head, axis, [((i + 1) % count, i) for i in range(count)]),
            ],
            axis=dim,
        )
    return cells


def laplace_padded(padded):
    center = padded[1:-1, 1:-1, 1:-1]
    total = padded[2:, 1:-1, 1:-1] + padded[:-2, 1:-1, 1:-1]
    total = total + padded[1:-1, 2:, 1:-1] + padded[1:-1, :-2, 1:-1]
    total = total + padded[1:-1, 1:-1, 2:] + padded[1:-1, 1:-1, :-2]
    return total - 6.0 * center


def flux_padded(values, mobility):
    center_v = values[1:-1, 1:-1, 1:-1]
    center_m = mobility[1:-1, 1:-1, 1:-1]
    total = jnp.zeros_like(center_v)
    pairs = (
        (
            values[2:, 1:-1, 1:-1],
            values[:-2, 1:-1, 1:-1],
            mobility[2:, 1:-1, 1:-1],
            mobility[:-2, 1:-1, 1:-1],
        ),
        (
            values[1:-1, 2:, 1:-1],
            values[1:-1, :-2, 1:-1],
            mobility[1:-1, 2:, 1:-1],
            mobility[1:-1, :-2, 1:-1],
        ),
        (
            values[1:-1, 1:-1, 2:],
            values[1:-1, 1:-1, :-2],
            mobility[1:-1, 1:-1, 2:],
            mobility[1:-1, 1:-1, :-2],
        ),
    )
    for upper_v, lower_v, upper_m, lower_m in pairs:
        total = (
            total
            + 0.5 * (upper_m + center_m) * (upper_v - center_v)
            - 0.5 * (center_m + lower_m) * (center_v - lower_v)
        )
    return total


def phase_update(phase_pad, centre_phase, centre_solute, centre_temp):
    square = 1.0 - centre_phase * centre_phase
    driving = (
        laplace_padded(phase_pad)
        + centre_phase
        - centre_phase * centre_phase * centre_phase
        - COUPLING * square * square * (centre_solute + centre_temp)
    )
    return jnp.clip(centre_phase + TIME_INCREMENT * driving, -1.0, 1.0)


def per_device(order_parameter, dissolved_species, broad_undercool):
    size_x, size_y, size_z = order_parameter.shape
    coarse_x = size_x // FACTOR
    coarse_y = size_y // FACTOR
    coarse_z = size_z // FACTOR
    start_x = lax.axis_index("gx") * coarse_x
    vertical_pile = broad_undercool
    for substep in range(SUBSTEPS):
        planes = lax.dynamic_slice_in_dim(vertical_pile, start_x, coarse_x, 2)
        local_col = jnp.transpose(planes, (2, 0, 1))
        fine_temp = jnp.repeat(jnp.repeat(jnp.repeat(local_col, FACTOR, 0), FACTOR, 1), FACTOR, 2)
        stacked = jnp.stack([order_parameter, dissolved_species])
        padded = padded_2(stacked, (("gx", 1), ("gy", 2), ("gz", 3)), 1)
        solute_pad = padded[1]
        new_phase = phase_update(padded[0], order_parameter, dissolved_species, fine_temp)
        new_pad = padded_2(new_phase, (("gx", 0), ("gy", 1), ("gz", 2)), 1)
        mobility = 0.5 * (1.0 - new_pad)
        change = new_phase - order_parameter
        numer = (
            TIME_INCREMENT * DIFFUSION * flux_padded(solute_pad, mobility)
            + 0.5 * (1.0 + (1.0 - PARTITION) * dissolved_species) * change
        )
        new_solute = dissolved_species + numer / (
            0.5 * (1.0 + PARTITION - (1.0 - PARTITION) * new_phase)
        )
        blocks = (0.5 * change).reshape(coarse_x, FACTOR, coarse_y, FACTOR, coarse_z, FACTOR)
        freezing_warmth_source = jnp.transpose(jnp.mean(blocks, axis=(1, 3, 5)), (1, 2, 0))
        heat_column = lax.all_gather(freezing_warmth_source, "gx", axis=2, tiled=True)
        col_pad = padded_2(vertical_pile, (("gy", 0), ("gz", 1)), 1)
        spread = (
            col_pad[2:, 1:-1, :]
            + col_pad[:-2, 1:-1, :]
            + col_pad[1:-1, 2:, :]
            + col_pad[1:-1, :-2, :]
        )
        spread = (
            spread
            + jnp.roll(vertical_pile, 1, 2)
            + jnp.roll(vertical_pile, -1, 2)
            - 6.0 * vertical_pile
        )
        vertical_pile = (
            vertical_pile + TIME_INCREMENT * THERMAL_SPREAD * spread + FREEZING_WARMTH * heat_column
        )
        order_parameter = new_phase
        dissolved_species = new_solute
    return (order_parameter, dissolved_species, vertical_pile)


def solution(mesh):
    return jax.shard_map(
        per_device,
        mesh=mesh,
        in_specs=(P("gx", "gy", "gz"), P("gx", "gy", "gz"), P("gy", "gz", None)),
        out_specs=(P("gx", "gy", "gz"), P("gx", "gy", "gz"), P("gy", "gz", None)),
        check_vma=False,
    )
```

profile of v0, /device:TPU:8, one launch (start us, length us, event | category | flops | bytes accessed | tf_op | source)
XLA Modules:
  0.0 411.6 jit_solution(16013132341941794809)
XLA Ops:
  1.9 6.9 %collective-permute-start.1 = (f32[2,1,128,128]{3,0,2,1:T(2,128)S(1)}, f32[2,1,128,128]{3,0,2,1:T(2,128)S(1)}, u32[]{:S(2)}, u32[]{:S(2)}) collective-permute-start(f32[2,1,128,128]{3,0,2,1:T(2,128)S(1)} %get-tuple-element.51), channel_id=1, source_target_pairs={{16,0},{32,16},{48,32},{64,48},{80,64},{96,80},{112,96},{128,112},... | collective-permute-start | bytes 393224 | tf_op jit(solution)/shard_map/ppermute | solution.py:27
  9.5 3.7 collective-permute-start.18
  17.7 3.9 collective-permute-start.3
  23.0 5.6 %collective-permute-done.2 = f32[2,6,1,128]{3,0,2,1:T(2,128)S(1)} collective-permute-done((f32[2,6,1,128]{3,0,2,1:T(2,128)S(1)}, f32[2,6,1,128]{3,0,2,1:T(2,128)S(1)}, u32[]{:S(2)}, u32[]{:S(2)}) %collective-permute-start.2) | collective-permute-done | bytes 6176 | tf_op jit(solution)/shard_map/ppermute | solution.py:25
  38.0 7.1 %pad_maximum_fusion.3 = f32[2,6,130,130]{3,0,2,1:T(2,128)S(1)} fusion(f32[2,6,130,1]{3,0,2,1:T(2,128)S(1)} %copy.85, f32[2,6,1,128]{3,0,2,1:T(2,128)S(1)} %collective-permute-done.3, f32[2,1,128,128]{3,0,2,1:T(2,128)S(1)} %collective-permute-done.1, f32[1,4,128,128]{3,0,2,1:T(1,128)S(1)} %bitcast.83, f32[1,4,128,128]{3,0,2,1:T(1,128)S(1)} %bitcast.79, ...), kind=kLoop, calls=%fused_computation.3 | loop fusion | flops 1419600 | bytes 1622400 | tf_op jit(solution)/shard_map/concatenate | solution.py:23
  45.2 2.1 fusion.160
  48.5 5.6 %collective-permute-start.7 = (f32[1,128,128]{2,1,0:T(8,128)}, f32[1,128,128]{2,1,0:T(8,128)S(1)}, u32[]{:S(2)}, u32[]{:S(2)}) collective-permute-start(f32[1,128,128]{2,1,0:T(8,128)} %get-tuple-element.111), channel_id=1, source_target_pairs={{16,0},{32,16},{48,32},{64,48},{80,64},{96,80},{112,96},{128,112},... | collective-permute-start | bytes 196616 | tf_op jit(solution)/shard_map/ppermute | solution.py:27
  54.1 2.1 reduce_sum.47
  56.5 44.0 %all_gather.12 = f32[32,32,16]{1,0,2:T(8,128)S(1)} all-gather(f32[32,32,1]{1,0,2:T(8,128)S(1)} %multiply_bitcast_fusion.3), channel_id=1, replica_groups=mesh['gx'=16,'gy'=4,'gz'=4] {'gx'}, dimensions={2}, use_global_device_ids=true | all-gather | bytes 69632 | tf_op jit(solution)/shard_map/all_gather | solution.py:113
  103.7 5.7 %collective-permute-done.8 = f32[6,1,128]{2,1,0:T(1,128)S(1)} collective-permute-done((f32[6,1,128]{2,1,0:T(1,128)S(1)}, f32[6,1,128]{2,1,0:T(1,128)S(1)}, u32[]{:S(2)}, u32[]{:S(2)}) %collective-permute-start.8) | collective-permute-done | bytes 3104 | tf_op jit(solution)/shard_map/ppermute | solution.py:25
  109.6 2.8 collective-permute-start.11
  114.8 3.1 collective-permute-done.11
  118.0 2.6 collective-permute-done.10
  123.0 2.0 collective-permute-start.12
  125.7 2.2 collective-permute-done.13
  127.9 4.0 collective-permute-done.12
  133.6 5.6 %collective-permute-done.14 = f32[2,6,1,128]{3,0,2,1:T(2,128)S(1)} collective-permute-done((f32[2,6,1,128]{3,0,2,1:T(2,128)S(1)}, f32[2,6,1,128]{3,0,2,1:T(2,128)S(1)}, u32[]{:S(2)}, u32[]{:S(2)}) %collective-permute-start.14) | collective-permute-done | bytes 6176 | tf_op jit(solution)/shard_map/ppermute | solution.py:25
  140.1 3.1 collective-permute-start.17
  144.7 2.0 collective-permute-start.36
  150.2 2.2 collective-permute-start.22
  152.4 3.5 reduce_sum.53
  157.7 42.1 %all_gather.13 = f32[32,32,16]{1,0,2:T(8,128)S(1)} all-gather(f32[32,32,1]{1,0,2:T(8,128)S(1)} %multiply_bitcast_fusion.2), channel_id=1, replica_groups=mesh['gx'=16,'gy'=4,'gz'=4] {'gx'}, dimensions={2}, use_global_device_ids=true | all-gather | bytes 69632 | tf_op jit(solution)/shard_map/all_gather | solution.py:113
  202.8 5.7 %collective-permute-done.24 = f32[6,1,128]{2,1,0:T(1,128)S(1)} collective-permute-done((f32[6,1,128]{2,1,0:T(1,128)S(1)}, f32[6,1,128]{2,1,0:T(1,128)S(1)}, u32[]{:S(2)}, u32[]{:S(2)}) %collective-permute-start.24) | collective-permute-done | bytes 3104 | tf_op jit(solution)/shard_map/ppermute | solution.py:25
  209.4 2.7 collective-permute-start.27
  213.5 5.9 %collective-permute-done.27 = f32[6,130,1]{2,1,0:T(8,128)S(1)} collective-permute-done((f32[6,130,1]{2,1,0:T(8,128)}, f32[6,130,1]{2,1,0:T(8,128)S(1)}, u32[]{:S(2)}, u32[]{:S(2)}) %collective-permute-start.27) | collective-permute-done | bytes 3152 | tf_op jit(solution)/shard_map/ppermute | solution.py:27
  219.4 2.0 collective-permute-done.26
  223.8 2.0 collective-permute-start.28
  226.6 2.2 collective-permute-done.29
  228.8 4.0 collective-permute-done.28
  234.2 5.7 %collective-permute-done.30 = f32[2,6,1,128]{3,0,2,1:T(2,128)S(1)} collective-permute-done((f32[2,6,1,128]{3,0,2,1:T(2,128)S(1)}, f32[2,6,1,128]{3,0,2,1:T(2,128)S(1)}, u32[]{:S(2)}, u32[]{:S(2)}) %collective-permute-start.30) | collective-permute-done | bytes 6176 | tf_op jit(solution)/shard_map/ppermute | solution.py:25
  243.8 2.0 fusion.170
  250.0 2.0 collective-permute-start.38
  252.0 3.5 reduce_sum.59
  257.4 42.1 %all_gather.14 = f32[32,32,16]{1,0,2:T(8,128)S(1)} all-gather(f32[32,32,1]{1,0,2:T(8,128)S(1)} %multiply_bitcast_fusion.1), channel_id=1, replica_groups=mesh['gx'=16,'gy'=4,'gz'=4] {'gx'}, dimensions={2}, use_global_device_ids=true | all-gather | bytes 69632 | tf_op jit(solution)/shard_map/all_gather | solution.py:113
  302.4 5.7 %collective-permute-done.40 = f32[6,1,128]{2,1,0:T(1,128)S(1)} collective-permute-done((f32[6,1,128]{2,1,0:T(1,128)S(1)}, f32[6,1,128]{2,1,0:T(1,128)S(1)}, u32[]{:S(2)}, u32[]{:S(2)}) %collective-permute-start.40) | collective-permute-done | bytes 3104 | tf_op jit(solution)/shard_map/ppermute | solution.py:25
  309.1 2.7 collective-permute-start.43
  313.9 4.2 %collective-permute-done.43 = f32[6,130,1]{2,1,0:T(8,128)S(1)} collective-permute-done((f32[6,130,1]{2,1,0:T(8,128)}, f32[6,130,1]{2,1,0:T(8,128)S(1)}, u32[]{:S(2)}, u32[]{:S(2)}) %collective-permute-start.43) | collective-permute-done | bytes 3152 | tf_op jit(solution)/shard_map/ppermute | solution.py:27
  318.0 2.0 collective-permute-done.42
  322.5 2.0 collective-permute-start.44
  325.2 2.2 collective-permute-done.45
  327.4 4.0 collective-permute-done.44
  332.9 5.7 %collective-permute-done.46 = f32[2,6,1,128]{3,0,2,1:T(2,128)S(1)} collective-permute-done((f32[2,6,1,128]{3,0,2,1:T(2,128)S(1)}, f32[2,6,1,128]{3,0,2,1:T(2,128)S(1)}, u32[]{:S(2)}, u32[]{:S(2)}) %collective-permute-start.46) | collective-permute-done | bytes 6176 | tf_op jit(solution)/shard_map/ppermute | solution.py:25
  348.1 2.2 collective-permute-start.54
  350.3 3.5 reduce_sum.74
  357.0 41.3 %all_gather.15 = f32[32,32,16]{1,0,2:T(8,128)S(1)} all-gather(f32[32,32,1]{1,0,2:T(8,128)S(1)} %multiply_bitcast_fusion), channel_id=1, replica_groups=mesh['gx'=16,'gy'=4,'gz'=4] {'gx'}, dimensions={2}, use_global_device_ids=true | all-gather | bytes 69632 | tf_op jit(solution)/shard_map/all_gather | solution.py:113
  398.6 2.7 collective-permute-start.59
  403.6 3.2 collective-permute-done.59
  406.9 2.5 collective-permute-done.58
  (276 shorter events, 84.0 us)
Async XLA Ops:
  1.9 14.0 %collective-permute-start.1 = (f32[2,1,128,128]{3,0,2,1:T(2,128)S(1)}, f32[2,1,128,128]{3,0,2,1:T(2,128)S(1)}, u32[]{:S(2)}, u32[]{:S(2)}) collective-permute-start(f32[2,1,128,128]{3,0,2,1:T(2,128)S(1)} %get-tuple-element.51), channel_id=1, source_target_pairs={{16,0},{32,16},{48,32},{64,48},{80,64},{96,80},{112,96},{128,112},... | collective-permute-start | bytes 393224 | tf_op jit(solution)/shard_map/ppermute | solution.py:27
  8.8 8.9 %collective-permute-start = (f32[2,1,128,128]{3,0,2,1:T(2,128)S(1)}, f32[2,1,128,128]{3,0,2,1:T(2,128)S(1)}, u32[]{:S(2)}, u32[]{:S(2)}) collective-permute-start(f32[2,1,128,128]{3,0,2,1:T(2,128)S(1)} %get-tuple-element.50), channel_id=1, source_target_pairs={{0,16},{16,32},{32,48},{48,64},{64,80},{80,96},{96,112},{112,128},... | collective-permute-start | bytes 393224 | tf_op jit(solution)/shard_map/ppermute | solution.py:25
  9.5 12.1 %collective-permute-start.18 = (f32[1,32,16]{1,0,2:T(1,128)S(1)}, f32[1,32,16]{1,0,2:T(1,128)S(1)}, u32[]{:S(2)}, u32[]{:S(2)}) collective-permute-start(f32[1,32,16]{1,0,2:T(1,128)S(1)} %bitcast.95), channel_id=1, source_target_pairs={{4,0},{8,4},{12,8},{0,12},{5,1},{9,5},{13,9},{1,13},{6,2},{10,6},{... | collective-permute-start | bytes 6152 | tf_op jit(solution)/shard_map/ppermute | solution.py:27
  13.2 8.5 %collective-permute-start.19 = (f32[1,32,16]{1,0,2:T(1,128)S(1)}, f32[1,32,16]{1,0,2:T(1,128)S(1)}, u32[]{:S(2)}, u32[]{:S(2)}) collective-permute-start(f32[1,32,16]{1,0,2:T(1,128)S(1)} %bitcast.94), channel_id=1, source_target_pairs={{0,4},{4,8},{8,12},{12,0},{1,5},{5,9},{9,13},{13,1},{2,6},{6,10},{... | collective-permute-start | bytes 6152 | tf_op jit(solution)/shard_map/ppermute | solution.py:25
  21.6 7.0 %collective-permute-start.2 = (f32[2,6,1,128]{3,0,2,1:T(2,128)S(1)}, f32[2,6,1,128]{3,0,2,1:T(2,128)S(1)}, u32[]{:S(2)}, u32[]{:S(2)}) collective-permute-start(f32[2,6,1,128]{3,0,2,1:T(2,128)S(1)} %get-tuple-element.42), channel_id=1, source_target_pairs={{0,4},{4,8},{8,12},{12,0},{1,5},{5,9},{9,13},{13,1},{2,6},{6,10},{... | collective-permute-start | bytes 18440 | tf_op jit(solution)/shard_map/ppermute | solution.py:25
  34.4 66.1 %collective-permute-start.21 = (f32[34,1,16]{1,0,2:T(8,128)}, f32[34,1,16]{1,0,2:T(8,128)}, u32[]{:S(2)}, u32[]{:S(2)}) collective-permute-start(f32[34,1,16]{1,0,2:T(8,128)} %get-tuple-element.75), channel_id=1, source_target_pairs={{0,1},{1,2},{2,3},{3,0},{4,5},{5,6},{6,7},{7,4},{8,9},{9,10},{10,1... | collective-permute-start | bytes 6536 | tf_op jit(solution)/shard_map/ppermute | solution.py:25
  36.0 64.6 %collective-permute-start.20 = (f32[34,1,16]{1,0,2:T(8,128)}, f32[34,1,16]{1,0,2:T(8,128)}, u32[]{:S(2)}, u32[]{:S(2)}) collective-permute-start(f32[34,1,16]{1,0,2:T(8,128)} %get-tuple-element.74), channel_id=1, source_target_pairs={{1,0},{2,1},{3,2},{0,3},{5,4},{6,5},{7,6},{4,7},{9,8},{10,9},{11,1... | collective-permute-start | bytes 6536 | tf_op jit(solution)/shard_map/ppermute | solution.py:27
  48.5 53.8 %collective-permute-start.7 = (f32[1,128,128]{2,1,0:T(8,128)}, f32[1,128,128]{2,1,0:T(8,128)S(1)}, u32[]{:S(2)}, u32[]{:S(2)}) collective-permute-start(f32[1,128,128]{2,1,0:T(8,128)} %get-tuple-element.111), channel_id=1, source_target_pairs={{16,0},{32,16},{48,32},{64,48},{80,64},{96,80},{112,96},{128,112},... | collective-permute-start | bytes 196616 | tf_op jit(solution)/shard_map/ppermute | solution.py:27
  54.1 48.1 %collective-permute-start.6 = (f32[1,128,128]{2,1,0:T(8,128)}, f32[1,128,128]{2,1,0:T(8,128)S(1)}, u32[]{:S(2)}, u32[]{:S(2)}) collective-permute-start(f32[1,128,128]{2,1,0:T(8,128)} %get-tuple-element.110), channel_id=1, source_target_pairs={{0,16},{16,32},{32,48},{48,64},{64,80},{80,96},{96,112},{112,128},... | collective-permute-start | bytes 196616 | tf_op jit(solution)/shard_map/ppermute | solution.py:25
  102.4 7.0 %collective-permute-start.8 = (f32[6,1,128]{2,1,0:T(1,128)S(1)}, f32[6,1,128]{2,1,0:T(1,128)S(1)}, u32[]{:S(2)}, u32[]{:S(2)}) collective-permute-start(f32[6,1,128]{2,1,0:T(1,128)S(1)} %get-tuple-element.66), channel_id=1, source_target_pairs={{0,4},{4,8},{8,12},{12,0},{1,5},{5,9},{9,13},{13,1},{2,6},{6,10},{... | collective-permute-start | bytes 9224 | tf_op jit(solution)/shard_map/ppermute | solution.py:25
  109.6 8.3 %collective-permute-start.11 = (f32[6,130,1]{2,1,0:T(8,128)S(1)}, f32[6,130,1]{2,1,0:T(8,128)S(1)}, u32[]{:S(2)}, u32[]{:S(2)}) collective-permute-start(f32[6,130,1]{2,1,0:T(8,128)S(1)} %get-tuple-element.59), channel_id=1, source_target_pairs={{1,0},{2,1},{3,2},{0,3},{5,4},{6,5},{7,6},{4,7},{9,8},{10,9},{11,1... | collective-permute-start | bytes 9368 | tf_op jit(solution)/shard_map/ppermute | solution.py:27
  112.4 8.1 %collective-permute-start.10 = (f32[6,130,1]{2,1,0:T(8,128)S(1)}, f32[6,130,1]{2,1,0:T(8,128)}, u32[]{:S(2)}, u32[]{:S(2)}) collective-permute-start(f32[6,130,1]{2,1,0:T(8,128)S(1)} %get-tuple-element.58), channel_id=1, source_target_pairs={{0,1},{1,2},{2,3},{3,0},{4,5},{5,6},{6,7},{7,4},{8,9},{9,10},{10,1... | collective-permute-start | bytes 9368 | tf_op jit(solution)/shard_map/ppermute | solution.py:25
  113.9 18.6 %collective-permute-start.34 = (f32[1,32,16]{1,0,2:T(1,128)}, f32[1,32,16]{1,0,2:T(1,128)S(1)}, u32[]{:S(2)}, u32[]{:S(2)}) collective-permute-start(f32[1,32,16]{1,0,2:T(1,128)} %get-tuple-element.100), channel_id=1, source_target_pairs={{4,0},{8,4},{12,8},{0,12},{5,1},{9,5},{13,9},{1,13},{6,2},{10,6},{... | collective-permute-start | bytes 6152 | tf_op jit(solution)/shard_map/ppermute | solution.py:27
  114.3 18.2 %collective-permute-start.35 = (f32[1,32,16]{1,0,2:T(1,128)}, f32[1,32,16]{1,0,2:T(1,128)S(1)}, u32[]{:S(2)}, u32[]{:S(2)}) collective-permute-start(f32[1,32,16]{1,0,2:T(1,128)} %get-tuple-element.99), channel_id=1, source_target_pairs={{0,4},{4,8},{8,12},{12,0},{1,5},{5,9},{9,13},{13,1},{2,6},{6,10},{... | collective-permute-start | bytes 6152 | tf_op jit(solution)/shard_map/ppermute | solution.py:25
  123.0 9.0 %collective-permute-start.12 = (f32[2,1,128,128]{3,2,1,0:T(8,128)S(1)}, f32[2,1,128,128]{3,2,1,0:T(8,128)S(1)}, u32[]{:S(2)}, u32[]{:S(2)}) collective-permute-start(f32[2,1,128,128]{3,2,1,0:T(8,128)S(1)} %get-tuple-element.48), channel_id=1, source_target_pairs={{0,16},{16,32},{32,48},{48,64},{64,80},{80,96},{96,112},{112,128},... | collective-permute-start | bytes 393224 | tf_op jit(solution)/shard_map/ppermute | solution.py:25
  132.3 7.0 %collective-permute-start.14 = (f32[2,6,1,128]{3,0,2,1:T(2,128)S(1)}, f32[2,6,1,128]{3,0,2,1:T(2,128)S(1)}, u32[]{:S(2)}, u32[]{:S(2)}) collective-permute-start(f32[2,6,1,128]{3,0,2,1:T(2,128)S(1)} %copy.90), channel_id=1, source_target_pairs={{0,4},{4,8},{8,12},{12,0},{1,5},{5,9},{9,13},{13,1},{2,6},{6,10},{... | collective-permute-start | bytes 18440 | tf_op jit(solution)/shard_map/ppermute | solution.py:25
  140.1 6.7 %collective-permute-start.17 = (f32[2,6,130,1]{2,0,3,1:T(2,128)S(1)}, f32[2,6,130,1]{2,0,3,1:T(2,128)S(1)}, u32[]{:S(2)}, u32[]{:S(2)}) collective-permute-start(f32[2,6,130,1]{2,0,3,1:T(2,128)S(1)} %copy.95), channel_id=1, source_target_pairs={{1,0},{2,1},{3,2},{0,3},{5,4},{6,5},{7,6},{4,7},{9,8},{10,9},{11,1... | collective-permute-start | bytes 18728 | tf_op jit(solution)/shard_map/ppermute | solution.py:27
  144.7 55.1 %collective-permute-start.37 = (f32[34,1,16]{1,0,2:T(8,128)}, f32[34,1,16]{1,0,2:T(8,128)}, u32[]{:S(2)}, u32[]{:S(2)}) collective-permute-start(f32[34,1,16]{1,0,2:T(8,128)} %get-tuple-element.73), channel_id=1, source_target_pairs={{0,1},{1,2},{2,3},{3,0},{4,5},{5,6},{6,7},{7,4},{8,9},{9,10},{10,1... | collective-permute-start | bytes 6536 | tf_op jit(solution)/shard_map/ppermute | solution.py:25
  144.7 55.1 %collective-permute-start.36 = (f32[34,1,16]{1,0,2:T(8,128)}, f32[34,1,16]{1,0,2:T(8,128)}, u32[]{:S(2)}, u32[]{:S(2)}) collective-permute-start(f32[34,1,16]{1,0,2:T(8,128)} %get-tuple-element.72), channel_id=1, source_target_pairs={{1,0},{2,1},{3,2},{0,3},{5,4},{6,5},{7,6},{4,7},{9,8},{10,9},{11,1... | collective-permute-start | bytes 6536 | tf_op jit(solution)/shard_map/ppermute | solution.py:27
  150.1 51.2 %collective-permute-start.23 = (f32[1,128,128]{2,1,0:T(8,128)S(1)}, f32[1,128,128]{2,1,0:T(8,128)S(1)}, u32[]{:S(2)}, u32[]{:S(2)}) collective-permute-start(f32[1,128,128]{2,1,0:T(8,128)S(1)} %get-tuple-element.102), channel_id=1, source_target_pairs={{16,0},{32,16},{48,32},{64,48},{80,64},{96,80},{112,96},{128,112},... | collective-permute-start | bytes 196616 | tf_op jit(solution)/shard_map/ppermute | solution.py:27
  150.2 51.1 %collective-permute-start.22 = (f32[1,128,128]{2,1,0:T(8,128)S(1)}, f32[1,128,128]{2,1,0:T(8,128)S(1)}, u32[]{:S(2)}, u32[]{:S(2)}) collective-permute-start(f32[1,128,128]{2,1,0:T(8,128)S(1)} %get-tuple-element.101), channel_id=1, source_target_pairs={{0,16},{16,32},{32,48},{48,64},{64,80},{80,96},{96,112},{112,128},... | collective-permute-start | bytes 196616 | tf_op jit(solution)/shard_map/ppermute | solution.py:25
  201.5 7.0 %collective-permute-start.24 = (f32[6,1,128]{2,1,0:T(1,128)S(1)}, f32[6,1,128]{2,1,0:T(1,128)S(1)}, u32[]{:S(2)}, u32[]{:S(2)}) collective-permute-start(f32[6,1,128]{2,1,0:T(1,128)S(1)} %get-tuple-element.64), channel_id=1, source_target_pairs={{0,4},{4,8},{8,12},{12,0},{1,5},{5,9},{9,13},{13,1},{2,6},{6,10},{... | collective-permute-start | bytes 9224 | tf_op jit(solution)/shard_map/ppermute | solution.py:25
  209.4 10.0 %collective-permute-start.27 = (f32[6,130,1]{2,1,0:T(8,128)}, f32[6,130,1]{2,1,0:T(8,128)S(1)}, u32[]{:S(2)}, u32[]{:S(2)}) collective-permute-start(f32[6,130,1]{2,1,0:T(8,128)} %get-tuple-element.57), channel_id=1, source_target_pairs={{1,0},{2,1},{3,2},{0,3},{5,4},{6,5},{7,6},{4,7},{9,8},{10,9},{11,1... | collective-permute-start | bytes 9368 | tf_op jit(solution)/shard_map/ppermute | solution.py:27
  212.1 9.3 %collective-permute-start.26 = (f32[6,130,1]{2,1,0:T(8,128)S(1)}, f32[6,130,1]{2,1,0:T(8,128)}, u32[]{:S(2)}, u32[]{:S(2)}) collective-permute-start(f32[6,130,1]{2,1,0:T(8,128)S(1)} %get-tuple-element.56), channel_id=1, source_target_pairs={{0,1},{1,2},{2,3},{3,0},{4,5},{5,6},{6,7},{7,4},{8,9},{9,10},{10,1... | collective-permute-start | bytes 9368 | tf_op jit(solution)/shard_map/ppermute | solution.py:25
  212.9 20.5 %collective-permute-start.50 = (f32[1,32,16]{1,0,2:T(1,128)S(1)}, f32[1,32,16]{1,0,2:T(1,128)S(1)}, u32[]{:S(2)}, u32[]{:S(2)}) collective-permute-start(f32[1,32,16]{1,0,2:T(1,128)S(1)} %get-tuple-element.91), channel_id=1, source_target_pairs={{4,0},{8,4},{12,8},{0,12},{5,1},{9,5},{13,9},{1,13},{6,2},{10,6},{... | collective-permute-start | bytes 6152 | tf_op jit(solution)/shard_map/ppermute | solution.py:27
  213.0 20.4 %collective-permute-start.51 = (f32[1,32,16]{1,0,2:T(1,128)S(1)}, f32[1,32,16]{1,0,2:T(1,128)S(1)}, u32[]{:S(2)}, u32[]{:S(2)}) collective-permute-start(f32[1,32,16]{1,0,2:T(1,128)S(1)} %get-tuple-element.90), channel_id=1, source_target_pairs={{0,4},{4,8},{8,12},{12,0},{1,5},{5,9},{9,13},{13,1},{2,6},{6,10},{... | collective-permute-start | bytes 6152 | tf_op jit(solution)/shard_map/ppermute | solution.py:25
  223.8 9.0 %collective-permute-start.28 = (f32[2,1,128,128]{3,2,1,0:T(8,128)S(1)}, f32[2,1,128,128]{3,2,1,0:T(8,128)S(1)}, u32[]{:S(2)}, u32[]{:S(2)}) collective-permute-start(f32[2,1,128,128]{3,2,1,0:T(8,128)S(1)} %get-tuple-element.46), channel_id=1, source_target_pairs={{0,16},{16,32},{32,48},{48,64},{64,80},{80,96},{96,112},{112,128},... | collective-permute-start | bytes 393224 | tf_op jit(solution)/shard_map/ppermute | solution.py:25
  232.9 7.0 %collective-permute-start.30 = (f32[2,6,1,128]{3,0,2,1:T(2,128)S(1)}, f32[2,6,1,128]{3,0,2,1:T(2,128)S(1)}, u32[]{:S(2)}, u32[]{:S(2)}) collective-permute-start(f32[2,6,1,128]{3,0,2,1:T(2,128)S(1)} %copy.113), channel_id=1, source_target_pairs={{0,4},{4,8},{8,12},{12,0},{1,5},{5,9},{9,13},{13,1},{2,6},{6,10},{... | collective-permute-start | bytes 18440 | tf_op jit(solution)/shard_map/ppermute | solution.py:25
  240.8 7.0 %collective-permute-start.33 = (f32[2,6,130,1]{2,0,3,1:T(2,128)S(1)}, f32[2,6,130,1]{2,0,3,1:T(2,128)S(1)}, u32[]{:S(2)}, u32[]{:S(2)}) collective-permute-start(f32[2,6,130,1]{2,0,3,1:T(2,128)S(1)} %copy.118), channel_id=1, source_target_pairs={{1,0},{2,1},{3,2},{0,3},{5,4},{6,5},{7,6},{4,7},{9,8},{10,9},{11,1... | collective-permute-start | bytes 18728 | tf_op jit(solution)/shard_map/ppermute | solution.py:27
  245.8 53.7 %collective-permute-start.53 = (f32[34,1,16]{1,0,2:T(8,128)}, f32[34,1,16]{1,0,2:T(8,128)}, u32[]{:S(2)}, u32[]{:S(2)}) collective-permute-start(f32[34,1,16]{1,0,2:T(8,128)} %get-tuple-element.71), channel_id=1, source_target_pairs={{0,1},{1,2},{2,3},{3,0},{4,5},{5,6},{6,7},{7,4},{8,9},{9,10},{10,1... | collective-permute-start | bytes 6536 | tf_op jit(solution)/shard_map/ppermute | solution.py:25
  246.1 53.4 %collective-permute-start.52 = (f32[34,1,16]{1,0,2:T(8,128)}, f32[34,1,16]{1,0,2:T(8,128)}, u32[]{:S(2)}, u32[]{:S(2)}) collective-permute-start(f32[34,1,16]{1,0,2:T(8,128)} %get-tuple-element.70), channel_id=1, source_target_pairs={{1,0},{2,1},{3,2},{0,3},{5,4},{6,5},{7,6},{4,7},{9,8},{10,9},{11,1... | collective-permute-start | bytes 6536 | tf_op jit(solution)/shard_map/ppermute | solution.py:27
  249.9 51.1 %collective-permute-start.39 = (f32[1,128,128]{2,1,0:T(8,128)S(1)}, f32[1,128,128]{2,1,0:T(8,128)S(1)}, u32[]{:S(2)}, u32[]{:S(2)}) collective-permute-start(f32[1,128,128]{2,1,0:T(8,128)S(1)} %get-tuple-element.93), channel_id=1, source_target_pairs={{16,0},{32,16},{48,32},{64,48},{80,64},{96,80},{112,96},{128,112},... | collective-permute-start | bytes 196616 | tf_op jit(solution)/shard_map/ppermute | solution.py:27
  250.0 51.0 %collective-permute-start.38 = (f32[1,128,128]{2,1,0:T(8,128)S(1)}, f32[1,128,128]{2,1,0:T(8,128)S(1)}, u32[]{:S(2)}, u32[]{:S(2)}) collective-permute-start(f32[1,128,128]{2,1,0:T(8,128)S(1)} %get-tuple-element.92), channel_id=1, source_target_pairs={{0,16},{16,32},{32,48},{48,64},{64,80},{80,96},{96,112},{112,128},... | collective-permute-start | bytes 196616 | tf_op jit(solution)/shard_map/ppermute | solution.py:25
  301.1 7.0 %collective-permute-start.40 = (f32[6,1,128]{2,1,0:T(1,128)S(1)}, f32[6,1,128]{2,1,0:T(1,128)S(1)}, u32[]{:S(2)}, u32[]{:S(2)}) collective-permute-start(f32[6,1,128]{2,1,0:T(1,128)S(1)} %get-tuple-element.62), channel_id=1, source_target_pairs={{0,4},{4,8},{8,12},{12,0},{1,5},{5,9},{9,13},{13,1},{2,6},{6,10},{... | collective-permute-start | bytes 9224 | tf_op jit(solution)/shard_map/ppermute | solution.py:25
  309.1 9.0 %collective-permute-start.43 = (f32[6,130,1]{2,1,0:T(8,128)}, f32[6,130,1]{2,1,0:T(8,128)S(1)}, u32[]{:S(2)}, u32[]{:S(2)}) collective-permute-start(f32[6,130,1]{2,1,0:T(8,128)} %get-tuple-element.55), channel_id=1, source_target_pairs={{1,0},{2,1},{3,2},{0,3},{5,4},{6,5},{7,6},{4,7},{9,8},{10,9},{11,1... | collective-permute-start | bytes 9368 | tf_op jit(solution)/shard_map/ppermute | solution.py:27
  311.8 8.3 %collective-permute-start.42 = (f32[6,130,1]{2,1,0:T(8,128)S(1)}, f32[6,130,1]{2,1,0:T(8,128)}, u32[]{:S(2)}, u32[]{:S(2)}) collective-permute-start(f32[6,130,1]{2,1,0:T(8,128)S(1)} %get-tuple-element.54), channel_id=1, source_target_pairs={{0,1},{1,2},{2,3},{3,0},{4,5},{5,6},{6,7},{7,4},{8,9},{9,10},{10,1... | collective-permute-start | bytes 9368 | tf_op jit(solution)/shard_map/ppermute | solution.py:25
  313.2 18.8 %collective-permute-start.60 = (f32[1,32,16]{1,0,2:T(1,128)S(1)}, f32[1,32,16]{1,0,2:T(1,128)S(1)}, u32[]{:S(2)}, u32[]{:S(2)}) collective-permute-start(f32[1,32,16]{1,0,2:T(1,128)S(1)} %get-tuple-element.82), channel_id=1, source_target_pairs={{4,0},{8,4},{12,8},{0,12},{5,1},{9,5},{13,9},{1,13},{6,2},{10,6},{... | collective-permute-start | bytes 6152 | tf_op jit(solution)/shard_map/ppermute | solution.py:27
  313.4 18.7 %collective-permute-start.61 = (f32[1,32,16]{1,0,2:T(1,128)S(1)}, f32[1,32,16]{1,0,2:T(1,128)S(1)}, u32[]{:S(2)}, u32[]{:S(2)}) collective-permute-start(f32[1,32,16]{1,0,2:T(1,128)S(1)} %get-tuple-element.81), channel_id=1, source_target_pairs={{0,4},{4,8},{8,12},{12,0},{1,5},{5,9},{9,13},{13,1},{2,6},{6,10},{... | collective-permute-start | bytes 6152 | tf_op jit(solution)/shard_map/ppermute | solution.py:25
  322.5 9.0 %collective-permute-start.44 = (f32[2,1,128,128]{3,2,1,0:T(8,128)S(1)}, f32[2,1,128,128]{3,2,1,0:T(8,128)S(1)}, u32[]{:S(2)}, u32[]{:S(2)}) collective-permute-start(f32[2,1,128,128]{3,2,1,0:T(8,128)S(1)} %get-tuple-element.44), channel_id=1, source_target_pairs={{0,16},{16,32},{32,48},{48,64},{64,80},{80,96},{96,112},{112,128},... | collective-permute-start | bytes 393224 | tf_op jit(solution)/shard_map/ppermute | solution.py:25
  331.6 7.0 %collective-permute-start.46 = (f32[2,6,1,128]{3,0,2,1:T(2,128)S(1)}, f32[2,6,1,128]{3,0,2,1:T(2,128)S(1)}, u32[]{:S(2)}, u32[]{:S(2)}) collective-permute-start(f32[2,6,1,128]{3,0,2,1:T(2,128)S(1)} %copy.125), channel_id=1, source_target_pairs={{0,4},{4,8},{8,12},{12,0},{1,5},{5,9},{9,13},{13,1},{2,6},{6,10},{... | collective-permute-start | bytes 18440 | tf_op jit(solution)/shard_map/ppermute | solution.py:25
  343.0 58.3 %collective-permute-start.63 = (f32[34,1,16]{1,0,2:T(8,128)}, f32[34,1,16]{1,0,2:T(8,128)S(1)}, u32[]{:S(2)}, u32[]{:S(2)}) collective-permute-start(f32[34,1,16]{1,0,2:T(8,128)} %get-tuple-element.69), channel_id=1, source_target_pairs={{0,1},{1,2},{2,3},{3,0},{4,5},{5,6},{6,7},{7,4},{8,9},{9,10},{10,1... | collective-permute-start | bytes 6536 | tf_op jit(solution)/shard_map/ppermute | solution.py:25
  343.3 58.1 %collective-permute-start.62 = (f32[34,1,16]{1,0,2:T(8,128)}, f32[34,1,16]{1,0,2:T(8,128)}, u32[]{:S(2)}, u32[]{:S(2)}) collective-permute-start(f32[34,1,16]{1,0,2:T(8,128)} %get-tuple-element.68), channel_id=1, source_target_pairs={{1,0},{2,1},{3,2},{0,3},{5,4},{6,5},{7,6},{4,7},{9,8},{10,9},{11,1... | collective-permute-start | bytes 6536 | tf_op jit(solution)/shard_map/ppermute | solution.py:27
  348.0 7.6 %collective-permute-start.55 = (f32[1,128,128]{2,1,0:T(8,128)S(1)}, f32[1,128,128]{2,1,0:T(8,128)S(1)}, u32[]{:S(2)}, u32[]{:S(2)}) collective-permute-start(f32[1,128,128]{2,1,0:T(8,128)S(1)} %get-tuple-element.84), channel_id=1, source_target_pairs={{16,0},{32,16},{48,32},{64,48},{80,64},{96,80},{112,96},{128,112},... | collective-permute-start | bytes 196616 | tf_op jit(solution)/shard_map/ppermute | solution.py:27
  348.1 8.5 %collective-permute-start.54 = (f32[1,128,128]{2,1,0:T(8,128)S(1)}, f32[1,128,128]{2,1,0:T(8,128)S(1)}, u32[]{:S(2)}, u32[]{:S(2)}) collective-permute-start(f32[1,128,128]{2,1,0:T(8,128)S(1)} %get-tuple-element.83), channel_id=1, source_target_pairs={{0,16},{16,32},{32,48},{48,64},{64,80},{80,96},{96,112},{112,128},... | collective-permute-start | bytes 196616 | tf_op jit(solution)/shard_map/ppermute | solution.py:25
  356.5 41.8 %collective-permute-start.57 = (f32[6,1,128]{2,1,0:T(1,128)S(1)}, f32[6,1,128]{2,1,0:T(1,128)S(1)}, u32[]{:S(2)}, u32[]{:S(2)}) collective-permute-start(f32[6,1,128]{2,1,0:T(1,128)S(1)} %get-tuple-element.61), channel_id=1, source_target_pairs={{4,0},{8,4},{12,8},{0,12},{5,1},{9,5},{13,9},{1,13},{6,2},{10,6},{... | collective-permute-start | bytes 9224 | tf_op jit(solution)/shard_map/ppermute | solution.py:27
  356.5 41.8 %collective-permute-start.56 = (f32[6,1,128]{2,1,0:T(1,128)S(1)}, f32[6,1,128]{2,1,0:T(1,128)S(1)}, u32[]{:S(2)}, u32[]{:S(2)}) collective-permute-start(f32[6,1,128]{2,1,0:T(1,128)S(1)} %get-tuple-element.60), channel_id=1, source_target_pairs={{0,4},{4,8},{8,12},{12,0},{1,5},{5,9},{9,13},{13,1},{2,6},{6,10},{... | collective-permute-start | bytes 9224 | tf_op jit(solution)/shard_map/ppermute | solution.py:25
  398.6 8.3 %collective-permute-start.59 = (f32[6,130,1]{2,1,0:T(8,128)S(1)}, f32[6,130,1]{2,1,0:T(8,128)S(1)}, u32[]{:S(2)}, u32[]{:S(2)}) collective-permute-start(f32[6,130,1]{2,1,0:T(8,128)S(1)} %get-tuple-element.53), channel_id=1, source_target_pairs={{1,0},{2,1},{3,2},{0,3},{5,4},{6,5},{7,6},{4,7},{9,8},{10,9},{11,1... | collective-permute-start | bytes 9368 | tf_op jit(solution)/shard_map/ppermute | solution.py:27
  401.3 8.0 %collective-permute-start.58 = (f32[6,130,1]{2,1,0:T(8,128)S(1)}, f32[6,130,1]{2,1,0:T(8,128)S(1)}, u32[]{:S(2)}, u32[]{:S(2)}) collective-permute-start(f32[6,130,1]{2,1,0:T(8,128)S(1)} %get-tuple-element.52), channel_id=1, source_target_pairs={{0,1},{1,2},{2,3},{3,0},{4,5},{5,6},{6,7},{7,4},{8,9},{9,10},{10,1... | collective-permute-start | bytes 9368 | tf_op jit(solution)/shard_map/ppermute | solution.py:25
  (44 other events, 849.2 us)
where the time goes:
time: 419 us; the launch traced here: 412 us
  blocking collectives  169 us (40%)
  waiting for transfers between devices  92.1 us (22%)
  starting transfers between devices  68.3 us (16%)
  local copies, waits for them, and re-layouts  44.4 us (11%)
  other arithmetic  35.4 us (8%)
    all_gather x4, blocking collectives, per_device(): lax.all_gather(freezing_warmth_source, 'gx', axis=2, tiled=True)  169 us
    ppermute x32, waiting for transfers between devices, padded_2(): lax.ppermute(tail, axis, [(i, (i + 1) % count) for i in range(count)])  64.2 us
    ppermute x32, starting transfers between devices, padded_2(): lax.ppermute(head, axis, [((i + 1) % count, i) for i in range(count)])  46.2 us
    ppermute x32, waiting for transfers between devices, padded_2(): lax.ppermute(head, axis, [((i + 1) % count, i) for i in range(count)])  27.9 us
    ppermute x32, starting transfers between devices, padded_2(): lax.ppermute(tail, axis, [(i, (i + 1) % count) for i in range(count)])  22.1 us
    reduce_sum x4, local copies, waits for them, and re-layouts, per_device(): jnp.mean(blocks, axis=(1, 3, 5))  12.5 us
    concatenate x16, other arithmetic, padded_2(): jnp.concatenate([lax.ppermute(tail, axis, [(i, (i + 1) % count) for i in...  11.3 us
  transfers between devices with their start and end apart: 64, of which 31 were waited for; matrix products, arithmetic and copies ran while one was open for 17% of the time, Pallas kernels for 0%

commit v1 on v0

v1 whole, which is shorter than its diff:
```python
import jax
import jax.numpy as jnp
from jax import lax
from jax.experimental import pallas as pl
from jax.experimental.pallas import tpu as pltpu
from jax.sharding import PartitionSpec as P

MESH = pl.DeviceIdType.MESH
HIGH = lax.Precision.HIGHEST
SUBSTEPS = 4
NGX, NGY, NGZ = 16, 4, 4
SX, SY, SZ = 4, 128, 128
CY = 32
PAD = 8
ROWS = 32


def lanes(shape):
    return lax.broadcasted_iota(jnp.int32, shape, len(shape) - 1)


def pack_plane(t):
    lane = lanes((8, 128))
    out = t[0:8]
    for k in range(1, 4):
        moved = pltpu.roll(t[8 * k : 8 * k + 8], 32 * k, 1)
        out = jnp.where(lane // 32 == k, moved, out)
    return out


def unpack_plane(tile):
    parts = [tile] + [pltpu.roll(tile, 128 - 32 * k, 1) for k in range(1, 4)]
    return jnp.concatenate(parts, axis=0)


def dot(a, b):
    return lax.dot_general(
        a, b, (((1,), (0,)), ((), ())), precision=HIGH, preferred_element_type=jnp.float32
    )


def kernel(
    phase_in, solute_in, temp_in,
    phase_out, solute_out, temp_out,
    ph, so, tcol, tp, fine,
    ysend, yrecv, zsend, zrecv,
    tsend, trecv, gath,
    load_sem,
    xp_s, xp_r, y_s, y_r, z_s, z_r, xu_s, xu_r, t_s, t_r, g_s, g_r,
):
    gx, gy, gz = lax.axis_index("gx"), lax.axis_index("gy"), lax.axis_index("gz")
    xdev = [{"gx": lax.rem(gx + NGX - 1, NGX)}, {"gx": lax.rem(gx + 1, NGX)}]
    ydev = [{"gy": lax.rem(gy + NGY - 1, NGY)}, {"gy": lax.rem(gy + 1, NGY)}]
    zdev = [{"gz": lax.rem(gz + NGZ - 1, NGZ)}, {"gz": lax.rem(gz + 1, NGZ)}]

    own = pl.ds(PAD, SY)
    loads = [
        pltpu.make_async_copy(phase_in, ph.at[0, pl.ds(1, SX), own], load_sem.at[0]),
        pltpu.make_async_copy(solute_in, so.at[0, pl.ds(1, SX), own], load_sem.at[1]),
        pltpu.make_async_copy(temp_in, tcol, load_sem.at[2]),
    ]
    for c in loads:
        c.start()

    barrier = pltpu.get_barrier_semaphore()
    for k in range(1, NGX):
        pl.semaphore_signal(
            barrier, inc=1, device_id={"gx": lax.rem(gx + k, NGX)}, device_id_type=MESH
        )
    for d in ydev + zdev:
        pl.semaphore_signal(barrier, inc=1, device_id=d, device_id_type=MESH)

    def remote(src, dst, s, r, dev):
        return pltpu.make_async_remote_copy(
            src_ref=src, dst_ref=dst, send_sem=s, recv_sem=r, device_id=dev, device_id_type=MESH
        )

    def xp_copy(slot, side):
        return remote(
            ph.at[slot, 1 if side == 0 else SX, own],
            ph.at[slot, SX + 1 if side == 0 else 0, own],
            xp_s.at[slot, side], xp_r.at[slot, side], xdev[side],
        )

    def xu_copy(slot, side):
        return remote(
            so.at[slot, 1 if side == 0 else SX, own],
            so.at[slot, SX + 1 if side == 0 else 0, own],
            xu_s.at[slot, side], xu_r.at[slot, side], xdev[side],
        )

    def y_copy(slot, side):
        return remote(
            ysend.at[slot, side], yrecv.at[slot, side], y_s.at[slot, side], y_r.at[slot, side], ydev[side]
        )

    def z_copy(slot, side):
        return remote(
            zsend.at[slot], zrecv.at[slot, side], z_s.at[slot, side], z_r.at[slot, side], zdev[side]
        )

    tdev = xdev + ydev + zdev

    def t_copy(slot, k):
        return remote(tsend.at[slot], trecv.at[slot, k], t_s.at[slot, k], t_r.at[slot, k], tdev[k])

    def g_copy(k):
        return remote(
            tsend.at[0], gath.at[gx], g_s.at[k], g_r.at[k], {"gx": lax.rem(gx + k, NGX)}
        )

    lane_z = lanes((SY, 128))

    def pack_y(pslot, uslot, slot):
        for side, row in ((0, PAD), (1, PAD + SY - 1)):
            for x in range(SX):
                ysend[slot, side, x : x + 1, :] = ph[pslot, x + 1, row : row + 1, :]
                ysend[slot, side, 4 + x : 5 + x, :] = so[uslot, x + 1, row : row + 1, :]

    def pack_z(pslot, uslot, slot):
        for c in range(SY // ROWS):
            lane = lanes((ROWS, 128))
            acc = jnp.zeros((ROWS, 128), jnp.float32)
            for x in range(SX):
                for f, (ref, sl) in enumerate(((ph, pslot), (so, uslot))):
                    v = ref[sl, x + 1, PAD + ROWS * c : PAD + ROWS * (c + 1), :]
                    l0 = x + 4 * f
                    acc = jnp.where(lane == l0, pltpu.roll(v, l0, 1) if l0 else v, acc)
                    acc = jnp.where(lane == l0 + 8, pltpu.roll(v, l0 + 9, 1), acc)
            zsend[slot, ROWS * c : ROWS * (c + 1), :] = acc

    def unpack_y(pslot, uslot, slot):
        for x in range(SX):
            ph[pslot, x + 1, PAD + SY : PAD + SY + 1, :] = yrecv[slot, 0, x : x + 1, :]
            ph[pslot, x + 1, PAD - 1 : PAD, :] = yrecv[slot, 1, x : x + 1, :]

    def unpack_yu(uslot, slot):
        for x in range(SX):
            so[uslot, x + 1, PAD + SY : PAD + SY + 1, :] = yrecv[slot, 0, 4 + x : 5 + x, :]
            so[uslot, x + 1, PAD - 1 : PAD, :] = yrecv[slot, 1, 4 + x : 5 + x, :]

    def z_neighbours(v, slot, rows, l0):
        lane = lanes(v.shape)
        upper = zrecv[slot, 0, rows, :]
        lower = zrecv[slot, 1, rows, :]
        vm = jnp.where(lane == 0, pltpu.roll(lower, 128 - (l0 + 8), 1), pltpu.roll(v, 1, 1))
        vp = jnp.where(lane == 127, pltpu.roll(upper, 127 - l0, 1), pltpu.roll(v, 127, 1))
        return vm, vp

    def phase_layer(x, old, new, uslot, slot):
        for c in range(SY // ROWS):
            r = PAD + ROWS * c
            rows = pl.ds(ROWS * c, ROWS)
            p = ph[old, x + 1, r : r + ROWS, :]
            zm, zp = z_neighbours(p, slot, rows, x)
            total = (
                (ph[old, x, r : r + ROWS, :] + ph[old, x + 2, r : r + ROWS, :])
                + (ph[old, x + 1, r - 1 : r + ROWS - 1, :] + ph[old, x + 1, r + 1 : r + ROWS + 1, :])
                + (zm + zp)
            )
            square = 1.0 - p * p
            drive = so[uslot, x + 1, r : r + ROWS, :] + fine[rows, :]
            driving = (total - 6.0 * p) + p * square - 3.0 * (square * square) * drive
            ph[new, x + 1, r : r + ROWS, :] = jnp.clip(p + 0.1 * driving, -1.0, 1.0)

    def solute_layer(x, old, new, slot):
        for c in range(SY // ROWS):
            r = PAD + ROWS * c
            rows = pl.ds(ROWS * c, ROWS)
            p = ph[new, x + 1, r : r + ROWS, :]
            u = so[old, x + 1, r : r + ROWS, :]
            q = 2.0 - p
            pzm, pzp = z_neighbours(p, slot, rows, x)
            uzm, uzp = z_neighbours(u, slot, rows, x + 4)
            flux = (q - pzm) * (uzm - u) + (q - pzp) * (uzp - u)
            for dx, dr in ((0, 0), (2, 0), (1, -1), (1, 1)):
                pn = ph[new, x + dx, r + dr : r + dr + ROWS, :]
                un = so[old, x + dx, r + dr : r + dr + ROWS, :]
                flux = flux + (q - pn) * (un - u)
            change = p - ph[old, x + 1, r : r + ROWS, :]
            numer = 0.05 * flux + (1.0 + 0.7 * u) * change
            so[new, x + 1, r : r + ROWS, :] = u + numer / (1.3 - 0.7 * p)

    zi = lax.broadcasted_iota(jnp.int32, (128, 128), 0)
    zj = lax.broadcasted_iota(jnp.int32, (128, 128), 1)
    spread_z = jnp.where(zj // 4 == zi, 1.0, 0.0).astype(jnp.float32)
    pool_z = jnp.where(zi // 4 == zj, 1.0, 0.0).astype(jnp.float32)
    yi = lax.broadcasted_iota(jnp.int32, (128, CY), 0)
    yj = lax.broadcasted_iota(jnp.int32, (128, CY), 1)
    spread_y = jnp.where(yi // 4 == yj, 1.0, 0.0).astype(jnp.float32)
    wi = lax.broadcasted_iota(jnp.int32, (CY, 128), 0)
    wj = lax.broadcasted_iota(jnp.int32, (CY, 128), 1)
    pool_y = jnp.where(wj // 4 == wi, 1.0, 0.0).astype(jnp.float32)

    def set_fine():
        fine[...] = dot(spread_y, dot(tp[...], spread_z))

    for c in loads:
        c.wait()
    pl.semaphore_wait(barrier, NGX - 1 + 4)
    for side in range(2):
        xp_copy(0, side).start()
    pack_y(0, 0, 0)
    for side in range(2):
        y_copy(0, side).start()
    pack_z(0, 0, 0)
    for side in range(2):
        z_copy(0, side).start()
    for side in range(2):
        xu_copy(0, side).start()
    tp[...] = jnp.zeros((CY, 128), jnp.float32)
    tp[:, 0:32] = tcol[:, pl.ds(gx, 1), :].reshape(CY, 32)
    tsend[0] = pack_plane(tp[...])
    for k in range(6):
        t_copy(0, k).start()
    set_fine()

    def wait_phase(slot):
        for side in range(2):
            xp_copy(slot, side).wait()
            y_copy(slot, side).wait()
            z_copy(slot, side).wait()

    wait_phase(0)
    unpack_y(0, 0, 0)

    lane_t = lanes((CY, 128))
    row_t = lax.broadcasted_iota(jnp.int32, (CY, 128), 0)

    def substep(s, carry):
        old = lax.rem(s, 2)
        new = 1 - old
        for x, side in ((0, 0), (3, 1)):
            phase_layer(x, old, new, old, old)
            xp_copy(new, side).start()
        for x in (1, 2):
            phase_layer(x, old, new, old, old)
        pack_y(new, old, new)
        for side in range(2):
            y_copy(new, side).start()
        pack_z(new, old, new)
        for side in range(2):
            z_copy(new, side).start()
        change = ph[new, 1, PAD : PAD + SY, :] - ph[old, 1, PAD : PAD + SY, :]
        for x in range(1, SX):
            change = change + (ph[new, x + 1, PAD : PAD + SY, :] - ph[old, x + 1, PAD : PAD + SY, :])
        heat = dot(pool_y, dot(change, pool_z))
        for k in range(6):
            t_copy(old, k).wait()
        t = tp[...]
        planes = [unpack_plane(trecv[old, k]) for k in range(6)]
        ym = jnp.where(row_t == 0, pltpu.roll(planes[3], 1, 0), pltpu.roll(t, 1, 0))
        yp = jnp.where(row_t == CY - 1, pltpu.roll(planes[2], CY - 1, 0), pltpu.roll(t, CY - 1, 0))
        zm = jnp.where(lane_t == 0, pltpu.roll(planes[5], 128 - 31, 1), pltpu.roll(t, 1, 1))
        zp = jnp.where(lane_t == 31, pltpu.roll(planes[4], 31, 1), pltpu.roll(t, 127, 1))
        total = (planes[0] + planes[1]) + (ym + yp) + (zm + zp) - 6.0 * t
        t = t + 0.12 * total + (2.0 * 0.5 / 64.0) * heat
        t = jnp.where(lane_t < 32, t, 0.0)
        tp[...] = t
        tsend[new] = pack_plane(t)

        @pl.when(s < SUBSTEPS - 1)
        def _():
            for k in range(6):
                t_copy(new, k).start()

        @pl.when(s == SUBSTEPS - 1)
        def _():
            for k in range(1, NGX):
                g_copy(k).start()

        set_fine()
        wait_phase(new)
        for side in range(2):
            xu_copy(old, side).wait()
        unpack_y(new, old, new)
        unpack_yu(old, new)
        for x, side in ((0, 0), (3, 1)):
            solute_layer(x, old, new, new)

            @pl.when(s < SUBSTEPS - 1)
            def _():
                xu_copy(new, side).start()

        for x in (1, 2):
            solute_layer(x, old, new, new)
        return carry

    lax.fori_loop(0, SUBSTEPS, substep, 0)

    outs = [
        pltpu.make_async_copy(ph.at[0, pl.ds(1, SX), own], phase_out, load_sem.at[0]),
        pltpu.make_async_copy(so.at[0, pl.ds(1, SX), own], solute_out, load_sem.at[1]),
    ]
    for c in outs:
        c.start()
    for k in range(1, NGX):
        g_copy(k).wait()
    gath[gx] = tsend[0]
    for x in range(NGX):
        temp_out[x] = unpack_plane(gath[x])[:, 0:32]
    for c in outs:
        c.wait()


def per_device(order_parameter, dissolved_species, broad_undercool):
    temp = jnp.transpose(broad_undercool, (0, 2, 1))
    f32 = jnp.float32
    dma = pltpu.SemaphoreType.DMA
    phase, solute, temp = pl.pallas_call(
        kernel,
        out_shape=(
            jax.ShapeDtypeStruct((SX, SY, SZ), f32),
            jax.ShapeDtypeStruct((SX, SY, SZ), f32),
            jax.ShapeDtypeStruct((NGX, CY, 32), f32),
        ),
        in_specs=[pl.BlockSpec(memory_space=pl.ANY)] * 3,
        out_specs=(
            pl.BlockSpec(memory_space=pl.ANY),
            pl.BlockSpec(memory_space=pl.ANY),
            pl.BlockSpec(memory_space=pltpu.VMEM),
        ),
        scratch_shapes=[
            pltpu.VMEM((2, SX + 2, SY + 2 * PAD, SZ), f32),
            pltpu.VMEM((2, SX + 2, SY + 2 * PAD, SZ), f32),
            pltpu.VMEM((CY, NGX, 32), f32),
            pltpu.VMEM((CY, 128), f32),
            pltpu.VMEM((SY, SZ), f32),
            pltpu.VMEM((2, 2, 8, 128), f32),
            pltpu.VMEM((2, 2, 8, 128), f32),
            pltpu.VMEM((2, SY, 128), f32),
            pltpu.VMEM((2, 2, SY, 128), f32),
            pltpu.VMEM((2, 8, 128), f32),
            pltpu.VMEM((2, 6, 8, 128), f32),
            pltpu.VMEM((NGX, 8, 128), f32),
            dma((3,)),
            dma((2, 2)), dma((2, 2)),
            dma((2, 2)), dma((2, 2)),
            dma((2, 2)), dma((2, 2)),
            dma((2, 2)), dma((2, 2)),
            dma((2, 6)), dma((2, 6)),
            dma((NGX,)), dma((NGX,)),
        ],
        compiler_params=pltpu.CompilerParams(
            collective_id=0, has_side_effects=True, vmem_limit_bytes=32 * 1024 * 1024
        ),
        name="solidify",
    )(order_parameter, dissolved_species, temp)
    return phase, solute, jnp.transpose(temp, (1, 2, 0))


def solution(mesh):
    specs = (P("gx", "gy", "gz"), P("gx", "gy", "gz"), P("gy", "gz", None))
    return jax.shard_map(
        per_device, mesh=mesh, in_specs=specs, out_specs=specs, check_vma=False
    )
```

time: 419 us -> 51.4 us (0.12)
  the two profiles are of different devices: /device:TPU:8 before, /device:TPU:1 now
where the time goes in v1:
time: 51.4 us; the launch traced here: 51.2 us
  Pallas kernels  45.4 us (88%)
  local copies, waits for them, and re-layouts  5.11 us (10%)
  between operations  0.65 us (1%)
    pallas_call x1, Pallas kernels, per_device(): pl.pallas_call(kernel, out_shape=(jax.ShapeDtypeStruct((SX, SY, SZ), f32)...  45.4 us
    unnamed x9, local copies, waits for them, and re-layouts  5.11 us

profile of v1, /device:TPU:1, one launch (start us, length us, event | category | flops | bytes accessed | tf_op | source)
XLA Modules:
  0.0 51.2 jit_solution(2787686515733537278)
XLA Ops:
  0.6 0.0 copy-start
  0.6 0.9 %copy-done = f32[4,128,128]{2,1,0:T(8,128)S(1)} copy-done((f32[4,128,128]{2,1,0:T(8,128)S(1)}, f32[4,128,128]{2,1,0:T(8,128)}, u32[]{:S(2)}) %copy-start) | copy-done | bytes 262168
  1.6 0.0 copy-start.1
  1.6 0.9 %copy-done.1 = f32[4,128,128]{2,1,0:T(8,128)S(1)} copy-done((f32[4,128,128]{2,1,0:T(8,128)S(1)}, f32[4,128,128]{2,1,0:T(8,128)}, u32[]{:S(2)}) %copy-start.1) | copy-done | bytes 262168
  2.5 0.0 copy-start.2
  2.5 0.9 %copy-done.2 = f32[32,32,16]{1,2,0:T(8,128)S(1)} copy-done((f32[32,32,16]{1,2,0:T(8,128)S(1)}, f32[32,32,16]{1,2,0:T(8,128)}, u32[]{:S(2)}) %copy-start.2) | copy-done | bytes 65560
  3.5 45.4 %solidify.1 = (f32[4,128,128]{2,1,0:T(8,128)S(1)}, f32[4,128,128]{2,1,0:T(8,128)S(1)}, f32[16,32,32]{2,1,0:T(8,128)S(1)}) custom-call(f32[4,128,128]{2,1,0:T(8,128)S(1)} %copy-done, f32[4,128,128]{2,1,0:T(8,128)S(1)} %copy-done.1, f32[32,16,32]{2,1,0:T(8,128)S(1)} %bitcast.2), custom_call_target="tpu_custom_call" | custom-call | tf_op jit(solution)/shard_map/solidify/pallas_call | solution.py:310
  48.9 0.9 %copy.6 = f32[32,32,16]{1,2,0:T(8,128)} copy(f32[32,32,16]{1,0,2:T(8,128)S(1)} %bitcast.3) | data formatting | bytes 131072
  49.8 0.7 %copy.9 = f32[4,128,128]{2,1,0:T(8,128)} copy(f32[4,128,128]{2,1,0:T(8,128)S(1)} %get-tuple-element.15) | data formatting | bytes 524288
  50.5 0.7 %copy.10 = f32[4,128,128]{2,1,0:T(8,128)} copy(f32[4,128,128]{2,1,0:T(8,128)S(1)} %get-tuple-element.16) | data formatting | bytes 524288
Async XLA Ops:
  0.6 1.0 %copy-start = (f32[4,128,128]{2,1,0:T(8,128)S(1)}, f32[4,128,128]{2,1,0:T(8,128)}, u32[]{:S(2)}) copy-start(f32[4,128,128]{2,1,0:T(8,128)} %phase_in.1) | copy-start | bytes 786436
  1.6 0.9 %copy-start.1 = (f32[4,128,128]{2,1,0:T(8,128)S(1)}, f32[4,128,128]{2,1,0:T(8,128)}, u32[]{:S(2)}) copy-start(f32[4,128,128]{2,1,0:T(8,128)} %solute_in.1) | copy-start | bytes 786436
  2.5 0.9 %copy-start.2 = (f32[32,32,16]{1,2,0:T(8,128)S(1)}, f32[32,32,16]{1,2,0:T(8,128)}, u32[]{:S(2)}) copy-start(f32[32,32,16]{1,2,0:T(8,128)} %param.5) | copy-start | bytes 196612

commit v2 on v1

v2 whole, which is shorter than its diff:
```python
import jax
import jax.numpy as jnp
from jax import lax
from jax.experimental import pallas as pl
from jax.experimental.pallas import tpu as pltpu
from jax.sharding import PartitionSpec as P

MESH = pl.DeviceIdType.MESH
HIGH = lax.Precision.HIGHEST
NGX, NGY, NGZ = 16, 4, 4
SX, SY, SZ = 4, 128, 128
CY = 32
PAD = 8
ROWS = 32
ORDER = (0, 3, 1, 2)
CHUNKS = SY // ROWS
PHASE, SOLUTE = 0, 1


def lanes(shape):
    return lax.broadcasted_iota(jnp.int32, shape, len(shape) - 1)


def roll(v, amount, axis=1):
    amount = amount % v.shape[axis]
    return pltpu.roll(v, amount, axis) if amount else v


def pack_plane(t):
    lane = lanes((8, 128))
    out = t[0:8]
    for k in range(1, 4):
        out = jnp.where(lane // 32 == k, roll(t[8 * k : 8 * k + 8], 32 * k), out)
    return out


def unpack_plane(tile):
    return jnp.concatenate([roll(tile, -32 * k) for k in range(4)], axis=0)


def dot(a, b):
    return lax.dot_general(
        a, b, (((1,), (0,)), ((), ())), precision=HIGH, preferred_element_type=jnp.float32
    )


def kernel(
    phase_in, solute_in, temp_in,
    phase_out, solute_out, temp_out,
    w, tcol, tp, fine,
    ysend, yrecv, zsend, zrecv, zhalo,
    tsend, trecv, gath,
    load_sem,
    x_s, x_r, y_s, y_r, z_s, z_r, t_s, t_r, g_s, g_r,
):
    gx, gy, gz = lax.axis_index("gx"), lax.axis_index("gy"), lax.axis_index("gz")
    xdev = [{"gx": lax.rem(gx + NGX - 1, NGX)}, {"gx": lax.rem(gx + 1, NGX)}]
    ydev = [{"gy": lax.rem(gy + NGY - 1, NGY)}, {"gy": lax.rem(gy + 1, NGY)}]
    zdev = [{"gz": lax.rem(gz + NGZ - 1, NGZ)}, {"gz": lax.rem(gz + 1, NGZ)}]
    tdev = xdev + ydev + zdev

    barrier = pltpu.get_barrier_semaphore()
    for k in range(1, NGX):
        pl.semaphore_signal(
            barrier, inc=1, device_id={"gx": lax.rem(gx + k, NGX)}, device_id_type=MESH
        )
    for d in ydev + zdev:
        pl.semaphore_signal(barrier, inc=1, device_id=d, device_id_type=MESH)

    own = pl.ds(PAD, SY)
    loads = [
        pltpu.make_async_copy(phase_in, w.at[0, pl.ds(1, SX), PHASE, own], load_sem.at[0]),
        pltpu.make_async_copy(solute_in, w.at[1, pl.ds(1, SX), SOLUTE, own], load_sem.at[1]),
        pltpu.make_async_copy(temp_in, tcol, load_sem.at[2]),
    ]
    for c in loads:
        c.start()

    def remote(src, dst, s, r, dev):
        return pltpu.make_async_remote_copy(
            src_ref=src, dst_ref=dst, send_sem=s, recv_sem=r, device_id=dev, device_id_type=MESH
        )

    def x_copy(slot, side, c, fields=pl.ds(0, 2)):
        rows = pl.ds(PAD + ROWS * c, ROWS)
        return remote(
            w.at[slot, 1 if side == 0 else SX, fields, rows],
            w.at[slot, SX + 1 if side == 0 else 0, fields, rows],
            x_s.at[slot, side, c], x_r.at[slot, side, c], xdev[side],
        )

    def y_copy(slot, side):
        return remote(
            ysend.at[slot, side], yrecv.at[slot, side], y_s.at[slot, side], y_r.at[slot, side], ydev[side]
        )

    def z_copy(slot, side):
        return remote(
            zsend.at[slot], zrecv.at[slot, side], z_s.at[slot, side], z_r.at[slot, side], zdev[side]
        )

    def t_copy(slot, k):
        return remote(tsend.at[slot], trecv.at[slot, k], t_s.at[slot, k], t_r.at[slot, k], tdev[k])

    def g_copy(k):
        return remote(
            tsend.at[0], gath.at[gx], g_s.at[k], g_r.at[k], {"gx": lax.rem(gx + k, NGX)}
        )

    def send_y(slot, fields=(PHASE, SOLUTE)):
        for side, row in ((0, PAD), (1, PAD + SY - 1)):
            for f in fields:
                for x in range(SX):
                    ysend[slot, side, 4 * f + x : 4 * f + x + 1, :] = w[slot, x + 1, f, row : row + 1, :]
            y_copy(slot, side).start()

    def send_z(slot, fields=(PHASE, SOLUTE)):
        lane = lanes((16, 128))
        acc = jnp.zeros((16, 128), jnp.float32)
        for g in range(8):
            for f in fields:
                for x in range(SX):
                    l0 = 16 * g + 2 * (x + 4 * f)
                    v = w[slot, x + 1, f, PAD + 16 * g : PAD + 16 * g + 16, :]
                    acc = jnp.where(lane // 2 == l0 // 2, roll(v, l0 + 1), acc)
        zsend[slot] = acc
        for side in range(2):
            z_copy(slot, side).start()

    def take_yz(slot, fields=(PHASE, SOLUTE)):
        for side in range(2):
            z_copy(slot, side).wait()
        lane = lanes((16, 128))
        zhalo[...] = jnp.where(
            lane % 2 == 0, roll(zrecv[slot, 0], -1), roll(zrecv[slot, 1], 1)
        )
        for side in range(2):
            y_copy(slot, side).wait()
        for f in fields:
            for x in range(SX):
                w[slot, x + 1, f, PAD + SY : PAD + SY + 1, :] = yrecv[slot, 0, 4 * f + x : 4 * f + x + 1, :]
                w[slot, x + 1, f, PAD - 1 : PAD, :] = yrecv[slot, 1, 4 * f + x : 4 * f + x + 1, :]

    def neighbours(slot, x, f, c):
        r = PAD + ROWS * c
        v = w[slot, x + 1, f, r : r + ROWS, :]
        lane = lanes((ROWS, 128))
        halo = jnp.concatenate(
            [roll(zhalo[...], 127 - (16 * g + 2 * (x + 4 * f))) for g in (2 * c, 2 * c + 1)], axis=0
        )
        return v, (
            w[slot, x, f, r : r + ROWS, :],
            w[slot, x + 2, f, r : r + ROWS, :],
            w[slot, x + 1, f, r - 1 : r + ROWS - 1, :],
            w[slot, x + 1, f, r + 1 : r + ROWS + 1, :],
            jnp.where(lane == 0, halo, roll(v, 1)),
            jnp.where(lane == 127, halo, roll(v, -1)),
        )

    def next_phase(p, near, u, c):
        total = (near[0] + near[1]) + (near[2] + near[3]) + (near[4] + near[5])
        square = 1.0 - p * p
        drive = u + fine[ROWS * c : ROWS * (c + 1), :]
        driving = (total - 6.0 * p) + p * square - 3.0 * (square * square) * drive
        return jnp.clip(p + 0.1 * driving, -1.0, 1.0)

    def next_solute(p, near, u, unear, before):
        q = 2.0 - p
        flux = (q - near[0]) * (unear[0] - u)
        for pn, un in zip(near[1:], unear[1:]):
            flux = flux + (q - pn) * (un - u)
        numer = 0.05 * flux + (1.0 + 0.7 * u) * (p - before)
        return u + numer / (1.3 - 0.7 * p)

    def first_phase(x, c):
        rows = pl.ds(PAD + ROWS * c, ROWS)
        p, near = neighbours(0, x, PHASE, c)
        w[1, x + 1, PHASE, rows, :] = next_phase(p, near, w[1, x + 1, SOLUTE, rows, :], c)

    def fused(x, c, a, b):
        rows = pl.ds(PAD + ROWS * c, ROWS)
        p, near = neighbours(a, x, PHASE, c)
        u, unear = neighbours(a, x, SOLUTE, c)
        u = next_solute(p, near, u, unear, w[b, x + 1, PHASE, rows, :])
        w[b, x + 1, SOLUTE, rows, :] = u
        w[b, x + 1, PHASE, rows, :] = next_phase(p, near, u, c)

    def last_solute(x, c):
        rows = pl.ds(PAD + ROWS * c, ROWS)
        p, near = neighbours(0, x, PHASE, c)
        u, unear = neighbours(0, x, SOLUTE, c)
        out = pl.ds(ROWS * c, ROWS)
        solute_out[x, out, :] = next_solute(p, near, u, unear, w[1, x + 1, PHASE, rows, :])
        phase_out[x, out, :] = p

    zi = lax.broadcasted_iota(jnp.int32, (128, 128), 0)
    zj = lax.broadcasted_iota(jnp.int32, (128, 128), 1)
    spread_z = jnp.where(zj // 4 == zi, 1.0, 0.0).astype(jnp.float32)
    pool_z = jnp.where(zi // 4 == zj, 1.0, 0.0).astype(jnp.float32)
    yi = lax.broadcasted_iota(jnp.int32, (128, CY), 0)
    yj = lax.broadcasted_iota(jnp.int32, (128, CY), 1)
    spread_y = jnp.where(yi // 4 == yj, 1.0, 0.0).astype(jnp.float32)
    wi = lax.broadcasted_iota(jnp.int32, (CY, 128), 0)
    wj = lax.broadcasted_iota(jnp.int32, (CY, 128), 1)
    pool_y = jnp.where(wj // 4 == wi, 1.0, 0.0).astype(jnp.float32)
    lane_t, row_t = wj, wi

    def set_fine():
        fine[...] = dot(spread_y, dot(tp[...], spread_z))

    def next_temp(a, b):
        change = w[b, 1, PHASE, own, :] - w[a, 1, PHASE, own, :]
        for x in range(1, SX):
            change = change + (w[b, x + 1, PHASE, own, :] - w[a, x + 1, PHASE, own, :])
        heat = dot(pool_y, dot(change, pool_z))
        for k in range(6):
            t_copy(a, k).wait()
        t = tp[...]
        planes = [unpack_plane(trecv[a, k]) for k in range(6)]
        ym = jnp.where(row_t == 0, roll(planes[3], 1, 0), roll(t, 1, 0))
        yp = jnp.where(row_t == CY - 1, roll(planes[2], -1, 0), roll(t, -1, 0))
        zm = jnp.where(lane_t == 0, roll(planes[5], -31), roll(t, 1))
        zp = jnp.where(lane_t == 31, roll(planes[4], 31), roll(t, -1))
        total = (planes[0] + planes[1]) + (ym + yp) + (zm + zp) - 6.0 * t
        t = t + 0.12 * total + (2.0 * 0.5 / 64.0) * heat
        t = jnp.where(lane_t < 32, t, 0.0)
        tp[...] = t
        tsend[b] = pack_plane(t)

    def layers(step, slot_in, slot_out, send, fields):
        for c in ORDER:
            for x in (1, 2):
                step(x, c)
        for c in ORDER:
            for x, side in ((0, 0), (3, 1)):
                x_copy(slot_in, 1 - side, c, fields).wait_recv()
                step(x, c)
                if send:
                    x_copy(slot_out, side, c).start()
            if send and c == ORDER[1]:
                send_y(slot_out)
        if send:
            send_z(slot_out)
        for c in ORDER:
            for side in range(2):
                x_copy(slot_in, side, c, fields).wait_send()

    only_phase = pl.ds(PHASE, 1)
    loads[0].wait()
    pl.semaphore_wait(barrier, NGX - 1 + 4)
    for c in ORDER:
        for side in range(2):
            x_copy(0, side, c, only_phase).start()
    ysend[...] = jnp.zeros_like(ysend)
    send_y(0, (PHASE,))
    send_z(0, (PHASE,))
    loads[2].wait()
    tp[...] = jnp.zeros((CY, 128), jnp.float32)
    tp[:, 0:32] = tcol[:, pl.ds(gx, 1), :].reshape(CY, 32)
    tsend[0] = pack_plane(tp[...])
    for k in range(6):
        t_copy(0, k).start()
    set_fine()
    loads[1].wait()
    take_yz(0, (PHASE,))
    layers(first_phase, 0, 1, True, only_phase)
    next_temp(0, 1)
    for k in range(6):
        t_copy(1, k).start()
    set_fine()

    def substep(r, carry):
        b = lax.rem(r, 2)
        a = 1 - b
        take_yz(a)
        layers(lambda x, c: fused(x, c, a, b), a, b, True, pl.ds(0, 2))
        next_temp(a, b)

        @pl.when(r < 4)
        def _():
            for k in range(6):
                t_copy(b, k).start()

        @pl.when(r == 4)
        def _():
            for k in range(1, NGX):
                g_copy(k).start()

        set_fine()
        return carry

    lax.fori_loop(2, 5, substep, 0)

    take_yz(0)
    layers(last_solute, 0, None, False, pl.ds(0, 2))
    for k in range(1, NGX):
        g_copy(k).wait()
    gath[gx] = tsend[0]
    for x in range(NGX):
        temp_out[:, x, :] = unpack_plane(gath[x])[:, 0:32]


def finish(phase, solute, temp, phase_out, solute_out, temp_out, sem):
    copies = [
        pltpu.make_async_copy(phase, phase_out, sem.at[0]),
        pltpu.make_async_copy(solute, solute_out, sem.at[1]),
        pltpu.make_async_copy(temp, temp_out, sem.at[2]),
    ]
    for c in copies:
        c.start()
    for c in copies:
        c.wait()


def per_device(order_parameter, dissolved_species, broad_undercool):
    temp = jnp.transpose(broad_undercool, (0, 2, 1))
    f32 = jnp.float32
    dma = pltpu.SemaphoreType.DMA
    vmem = pl.BlockSpec(memory_space=pltpu.VMEM)
    hbm = pl.BlockSpec(memory_space=pltpu.HBM)
    block = jax.ShapeDtypeStruct((SX, SY, SZ), f32)
    phase, solute, temp = pl.pallas_call(
        kernel,
        out_shape=(block, block, jax.ShapeDtypeStruct((CY, NGX, 32), f32)),
        in_specs=[hbm] * 3,
        out_specs=(vmem, vmem, vmem),
        scratch_shapes=[
            pltpu.VMEM((2, SX + 2, 2, SY + 2 * PAD, SZ), f32),
            pltpu.VMEM((CY, NGX, 32), f32),
            pltpu.VMEM((CY, 128), f32),
            pltpu.VMEM((SY, SZ), f32),
            pltpu.VMEM((2, 2, 8, 128), f32),
            pltpu.VMEM((2, 2, 8, 128), f32),
            pltpu.VMEM((2, 16, 128), f32),
            pltpu.VMEM((2, 2, 16, 128), f32),
            pltpu.VMEM((16, 128), f32),
            pltpu.VMEM((2, 8, 128), f32),
            pltpu.VMEM((2, 6, 8, 128), f32),
            pltpu.VMEM((NGX, 8, 128), f32),
            dma((3,)),
            dma((2, 2, CHUNKS)), dma((2, 2, CHUNKS)),
            dma((2, 2)), dma((2, 2)),
            dma((2, 2)), dma((2, 2)),
            dma((2, 6)), dma((2, 6)),
            dma((NGX,)), dma((NGX,)),
        ],
        compiler_params=pltpu.CompilerParams(
            collective_id=0, has_side_effects=True, vmem_limit_bytes=54300 * 1024
        ),
        name="solidify",
    )(order_parameter, dissolved_species, temp)
    phase, solute, temp = pl.pallas_call(
        finish,
        out_shape=(block, block, jax.ShapeDtypeStruct((CY, NGX, 32), f32)),
        in_specs=[pl.BlockSpec(memory_space=pl.ANY)] * 3,
        out_specs=(hbm, hbm, hbm),
        scratch_shapes=[dma((3,))],
        compiler_params=pltpu.CompilerParams(vmem_limit_bytes=1024 * 1024),
        name="finish",
    )(phase, solute, temp)
    return phase, solute, jnp.transpose(temp, (0, 2, 1))


def solution(mesh):
    specs = (P("gx", "gy", "gz"), P("gx", "gy", "gz"), P("gy", "gz", None))
    return jax.shard_map(
        per_device, mesh=mesh, in_specs=specs, out_specs=specs, check_vma=False
    )
```

time: 51.4 us -> 43.8 us (0.85)
  local copies, waits for them, and re-layouts: 5.11 us -> 0 us
  Pallas kernels: 45.4 us -> 43 us
    unnamed x9 -> x0, local copies, waits for them, and re-layouts: 5.11 us -> none
    pallas_call x1 -> x2, Pallas kernels: 45.4 us -> 43 us  [the longest x1 42.1 us: per_device(): pl.pallas_call(kernel, out_shape=(block, block, jax.ShapeDtypeStruct((CY,...]
where the time goes in v2:
time: 43.8 us; the launch traced here: 43.7 us
  Pallas kernels  43 us (98%)
  between operations  0.64 us (1%)
    pallas_call x1, Pallas kernels, per_device(): pl.pallas_call(kernel, out_shape=(block, block, jax.ShapeDtypeStruct((CY,...  42.1 us
    pallas_call x1, Pallas kernels, per_device(): pl.pallas_call(finish, out_shape=(block, block, jax.ShapeDtypeStruct((CY,...  0.9 us

profile of v2, /device:TPU:1, one launch (start us, length us, event | category | flops | bytes accessed | tf_op | source)
XLA Modules:
  0.0 43.7 jit_solution(10064292722579483796)
XLA Ops:
  0.6 42.1 %solidify.1 = (f32[4,128,128]{2,1,0:T(8,128)S(1)}, f32[4,128,128]{2,1,0:T(8,128)S(1)}, f32[32,16,32]{2,1,0:T(8,128)S(1)}) custom-call(f32[4,128,128]{2,1,0:T(8,128)} %phase_in.1, f32[4,128,128]{2,1,0:T(8,128)} %solute_in.1, f32[32,16,32]{2,1,0:T(8,128)} %bitcast.2), custom_call_target="tpu_custom_call" | custom-call | tf_op jit(solution)/shard_map/solidify/pallas_call | solution.py:322
  42.8 0.9 %finish.1 = (f32[4,128,128]{2,1,0:T(8,128)}, f32[4,128,128]{2,1,0:T(8,128)}, f32[32,16,32]{2,1,0:T(8,128)}) custom-call(f32[4,128,128]{2,1,0:T(8,128)S(1)} %get-tuple-element.9.phase, f32[4,128,128]{2,1,0:T(8,128)S(1)} %get-tuple-element.10.solute, f32[32,16,32]{2,1,0:T(8,128)S(1)} %get-tuple-element.11.temp), custom_call_target="tpu_custom_call" | custom-call | tf_op jit(solution)/shard_map/finish/pallas_call | solution.py:352

commit v3 on v2

--- a/solution.py
+++ b/solution.py
@@ -11,9 +11,8 @@
 SX, SY, SZ = 4, 128, 128
 CY = 32
 PAD = 8
-ROWS = 32
-ORDER = (0, 3, 1, 2)
-CHUNKS = SY // ROWS
+PIECES = ((0, 8), (120, 8), (8, 32), (40, 32), (72, 48))
+EDGES = 2
 PHASE, SOLUTE = 0, 1
 
 
@@ -48,10 +47,10 @@
     phase_in, solute_in, temp_in,
     phase_out, solute_out, temp_out,
     w, tcol, tp, fine,
-    ysend, yrecv, zsend, zrecv, zhalo,
+    ysend, yrecv, esend, erecv, ehalo, zsend, zrecv, zhalo,
     tsend, trecv, gath,
     load_sem,
-    x_s, x_r, y_s, y_r, z_s, z_r, t_s, t_r, g_s, g_r,
+    x_s, x_r, y_s, y_r, e_s, e_r, z_s, z_r, t_s, t_r, g_s, g_r,
 ):
     gx, gy, gz = lax.axis_index("gx"), lax.axis_index("gy"), lax.axis_index("gz")
     xdev = [{"gx": lax.rem(gx + NGX - 1, NGX)}, {"gx": lax.rem(gx + 1, NGX)}]
@@ -82,7 +81,7 @@
         )
 
     def x_copy(slot, side, c, fields=pl.ds(0, 2)):
-        rows = pl.ds(PAD + ROWS * c, ROWS)
+        rows = pl.ds(PAD + PIECES[c][0], PIECES[c][1])
         return remote(
             w.at[slot, 1 if side == 0 else SX, fields, rows],
             w.at[slot, SX + 1 if side == 0 else 0, fields, rows],
@@ -97,6 +96,11 @@
     def z_copy(slot, side):
         return remote(
             zsend.at[slot], zrecv.at[slot, side], z_s.at[slot, side], z_r.at[slot, side], zdev[side]
+        )
+
+    def e_copy(slot, side):
+        return remote(
+            esend.at[slot], erecv.at[slot, side], e_s.at[slot, side], e_r.at[slot, side], zdev[side]
         )
 
     def t_copy(slot, k):
@@ -114,26 +118,34 @@
                     ysend[slot, side, 4 * f + x : 4 * f + x + 1, :] = w[slot, x + 1, f, row : row + 1, :]
             y_copy(slot, side).start()
 
-    def send_z(slot, fields=(PHASE, SOLUTE)):
-        lane = lanes((16, 128))
-        acc = jnp.zeros((16, 128), jnp.float32)
-        for g in range(8):
+    def pack_z(slot, fields, groups, height):
+        lane = lanes((height, 128))
+        acc = jnp.zeros((height, 128), jnp.float32)
+        for k, first in enumerate(groups):
             for f in fields:
                 for x in range(SX):
-                    l0 = 16 * g + 2 * (x + 4 * f)
-                    v = w[slot, x + 1, f, PAD + 16 * g : PAD + 16 * g + 16, :]
+                    l0 = 16 * k + 2 * (x + 4 * f)
+                    v = w[slot, x + 1, f, PAD + first : PAD + first + height, :]
                     acc = jnp.where(lane // 2 == l0 // 2, roll(v, l0 + 1), acc)
-        zsend[slot] = acc
+        return acc
+
+    def send_edge_z(slot, fields=(PHASE, SOLUTE)):
+        esend[slot] = pack_z(slot, fields, (0, SY - 8), 8)
+        for side in range(2):
+            e_copy(slot, side).start()
+
+    def send_z(slot, fields=(PHASE, SOLUTE)):
+        zsend[slot] = pack_z(slot, fields, range(8, SY - 8, 16), 16)
         for side in range(2):
             z_copy(slot, side).start()
 
-    def take_yz(slot, fields=(PHASE, SOLUTE)):
-        for side in range(2):
-            z_copy(slot, side).wait()
-        lane = lanes((16, 128))
-        zhalo[...] = jnp.where(
-            lane % 2 == 0, roll(zrecv[slot, 0], -1), roll(zrecv[slot, 1], 1)
-        )
+    def swap_z(upper, lower):
+        return jnp.where(lanes(upper.shape) % 2 == 0, roll(upper, -1), roll(lower, 1))
+
+    def take_edges(slot, fields=(PHASE, SOLUTE)):
+        for side in range(2):
+            e_copy(slot, side).wait()
+        ehalo[...] = swap_z(erecv[slot, 0], erecv[slot, 1])
         for side in range(2):
             y_copy(slot, side).wait()
         for f in fields:
@@ -141,18 +153,27 @@
                 w[slot, x + 1, f, PAD + SY : PAD + SY + 1, :] = yrecv[slot, 0, 4 * f + x : 4 * f + x + 1, :]
                 w[slot, x + 1, f, PAD - 1 : PAD, :] = yrecv[slot, 1, 4 * f + x : 4 * f + x + 1, :]
 
+    def take_z(slot):
+        for side in range(2):
+            z_copy(slot, side).wait()
+        zhalo[...] = swap_z(zrecv[slot, 0], zrecv[slot, 1])
+
     def neighbours(slot, x, f, c):
-        r = PAD + ROWS * c
-        v = w[slot, x + 1, f, r : r + ROWS, :]
-        lane = lanes((ROWS, 128))
-        halo = jnp.concatenate(
-            [roll(zhalo[...], 127 - (16 * g + 2 * (x + 4 * f))) for g in (2 * c, 2 * c + 1)], axis=0
-        )
+        first, count = PIECES[c]
+        r = PAD + first
+        v = w[slot, x + 1, f, r : r + count, :]
+        lane = lanes((count, 128))
+        j = 2 * (x + 4 * f)
+        if c < EDGES:
+            halo = roll(ehalo[...], 127 - (16 * c + j))
+        else:
+            groups = range((first - 8) // 16, (first + count - 8) // 16)
+            halo = jnp.concatenate([roll(zhalo[...], 127 - (16 * g + j)) for g in groups], axis=0)
         return v, (
-            w[slot, x, f, r : r + ROWS, :],
-            w[slot, x + 2, f, r : r + ROWS, :],
-            w[slot, x + 1, f, r - 1 : r + ROWS - 1, :],
-            w[slot, x + 1, f, r + 1 : r + ROWS + 1, :],
+            w[slot, x, f, r : r + count, :],
+            w[slot, x + 2, f, r : r + count, :],
+            w[slot, x + 1, f, r - 1 : r + count - 1, :],
+            w[slot, x + 1, f, r + 1 : r + count + 1, :],
             jnp.where(lane == 0, halo, roll(v, 1)),
             jnp.where(lane == 127, halo, roll(v, -1)),
         )
@@ -160,7 +181,7 @@
     def next_phase(p, near, u, c):
         total = (near[0] + near[1]) + (near[2] + near[3]) + (near[4] + near[5])
         square = 1.0 - p * p
-        drive = u + fine[ROWS * c : ROWS * (c + 1), :]
+        drive = u + fine[PIECES[c][0] : PIECES[c][0] + PIECES[c][1], :]
         driving = (total - 6.0 * p) + p * square - 3.0 * (square * square) * drive
         return jnp.clip(p + 0.1 * driving, -1.0, 1.0)
 
@@ -173,12 +194,12 @@
         return u + numer / (1.3 - 0.7 * p)
 
     def first_phase(x, c):
-        rows = pl.ds(PAD + ROWS * c, ROWS)
+        rows = pl.ds(PAD + PIECES[c][0], PIECES[c][1])
         p, near = neighbours(0, x, PHASE, c)
         w[1, x + 1, PHASE, rows, :] = next_phase(p, near, w[1, x + 1, SOLUTE, rows, :], c)
 
     def fused(x, c, a, b):
-        rows = pl.ds(PAD + ROWS * c, ROWS)
+        rows = pl.ds(PAD + PIECES[c][0], PIECES[c][1])
         p, near = neighbours(a, x, PHASE, c)
         u, unear = neighbours(a, x, SOLUTE, c)
         u = next_solute(p, near, u, unear, w[b, x + 1, PHASE, rows, :])
@@ -186,10 +207,10 @@
         w[b, x + 1, PHASE, rows, :] = next_phase(p, near, u, c)
 
     def last_solute(x, c):
-        rows = pl.ds(PAD + ROWS * c, ROWS)
+        rows = pl.ds(PAD + PIECES[c][0], PIECES[c][1])
         p, near = neighbours(0, x, PHASE, c)
         u, unear = neighbours(0, x, SOLUTE, c)
-        out = pl.ds(ROWS * c, ROWS)
+        out = pl.ds(*PIECES[c])
         solute_out[x, out, :] = next_solute(p, near, u, unear, w[1, x + 1, PHASE, rows, :])
         phase_out[x, out, :] = p
 
@@ -228,31 +249,36 @@
         tsend[b] = pack_plane(t)
 
     def layers(step, slot_in, slot_out, send, fields):
-        for c in ORDER:
+        taken = (PHASE, SOLUTE) if fields.size == 2 else (PHASE,)
+        take_edges(slot_in, taken)
+        for c in range(len(PIECES)):
+            if c == EDGES:
+                take_z(slot_in)
             for x in (1, 2):
                 step(x, c)
-        for c in ORDER:
             for x, side in ((0, 0), (3, 1)):
                 x_copy(slot_in, 1 - side, c, fields).wait_recv()
                 step(x, c)
                 if send:
                     x_copy(slot_out, side, c).start()
-            if send and c == ORDER[1]:
+            if send and c == EDGES - 1:
                 send_y(slot_out)
+                send_edge_z(slot_out)
         if send:
             send_z(slot_out)
-        for c in ORDER:
+        for c in range(len(PIECES)):
             for side in range(2):
                 x_copy(slot_in, side, c, fields).wait_send()
 
     only_phase = pl.ds(PHASE, 1)
     loads[0].wait()
     pl.semaphore_wait(barrier, NGX - 1 + 4)
-    for c in ORDER:
+    for c in range(len(PIECES)):
         for side in range(2):
             x_copy(0, side, c, only_phase).start()
     ysend[...] = jnp.zeros_like(ysend)
     send_y(0, (PHASE,))
+    send_edge_z(0, (PHASE,))
     send_z(0, (PHASE,))
     loads[2].wait()
     tp[...] = jnp.zeros((CY, 128), jnp.float32)
@@ -262,7 +288,6 @@
         t_copy(0, k).start()
     set_fine()
     loads[1].wait()
-    take_yz(0, (PHASE,))
     layers(first_phase, 0, 1, True, only_phase)
     next_temp(0, 1)
     for k in range(6):
@@ -272,7 +297,6 @@
     def substep(r, carry):
         b = lax.rem(r, 2)
         a = 1 - b
-        take_yz(a)
         layers(lambda x, c: fused(x, c, a, b), a, b, True, pl.ds(0, 2))
         next_temp(a, b)
 
@@ -291,7 +315,6 @@
 
     lax.fori_loop(2, 5, substep, 0)
 
-    take_yz(0)
     layers(last_solute, 0, None, False, pl.ds(0, 2))
     for k in range(1, NGX):
         g_copy(k).wait()
@@ -331,6 +354,9 @@
             pltpu.VMEM((SY, SZ), f32),
             pltpu.VMEM((2, 2, 8, 128), f32),
             pltpu.VMEM((2, 2, 8, 128), f32),
+            pltpu.VMEM((2, 8, 128), f32),
+            pltpu.VMEM((2, 2, 8, 128), f32),
+            pltpu.VMEM((8, 128), f32),
             pltpu.VMEM((2, 16, 128), f32),
             pltpu.VMEM((2, 2, 16, 128), f32),
             pltpu.VMEM((16, 128), f32),
@@ -338,7 +364,8 @@
             pltpu.VMEM((2, 6, 8, 128), f32),
             pltpu.VMEM((NGX, 8, 128), f32),
             dma((3,)),
-            dma((2, 2, CHUNKS)), dma((2, 2, CHUNKS)),
+            dma((2, 2, len(PIECES))), dma((2, 2, len(PIECES))),
+            dma((2, 2)), dma((2, 2)),
             dma((2, 2)), dma((2, 2)),
             dma((2, 2)), dma((2, 2)),
             dma((2, 6)), dma((2, 6)),

time: 43.8 us -> 41 us (0.936)
  Pallas kernels: 43 us -> 40.2 us
    pallas_call x1, Pallas kernels: 42.1 us -> 39.3 us  [per_device(): pl.pallas_call(kernel, out_shape=(block, block, jax.ShapeDtypeStruct((CY,...]
where the time goes in v3:
time: 41 us; the launch traced here: 40.9 us
  Pallas kernels  40.2 us (98%)
  between operations  0.64 us (2%)
    pallas_call x1, Pallas kernels, per_device(): pl.pallas_call(kernel, out_shape=(block, block, jax.ShapeDtypeStruct((CY,...  39.3 us
    pallas_call x1, Pallas kernels, per_device(): pl.pallas_call(finish, out_shape=(block, block, jax.ShapeDtypeStruct((CY,...  0.9 us

profile of v3, /device:TPU:1, one launch (start us, length us, event | category | flops | bytes accessed | tf_op | source)
XLA Modules:
  0.0 40.9 jit_solution(3809026319710898002)
XLA Ops:
  0.6 39.3 %solidify.1 = (f32[4,128,128]{2,1,0:T(8,128)S(1)}, f32[4,128,128]{2,1,0:T(8,128)S(1)}, f32[32,16,32]{2,1,0:T(8,128)S(1)}) custom-call(f32[4,128,128]{2,1,0:T(8,128)} %phase_in.1, f32[4,128,128]{2,1,0:T(8,128)} %solute_in.1, f32[32,16,32]{2,1,0:T(8,128)} %bitcast.2), custom_call_target="tpu_custom_call" | custom-call | tf_op jit(solution)/shard_map/solidify/pallas_call | solution.py:345
  40.0 0.9 %finish.1 = (f32[4,128,128]{2,1,0:T(8,128)}, f32[4,128,128]{2,1,0:T(8,128)}, f32[32,16,32]{2,1,0:T(8,128)}) custom-call(f32[4,128,128]{2,1,0:T(8,128)S(1)} %get-tuple-element.9.phase, f32[4,128,128]{2,1,0:T(8,128)S(1)} %get-tuple-element.10.solute, f32[32,16,32]{2,1,0:T(8,128)S(1)} %get-tuple-element.11.temp), custom_call_target="tpu_custom_call" | custom-call | tf_op jit(solution)/shard_map/finish/pallas_call | solution.py:379

commit v4 on v3

--- a/solution.py
+++ b/solution.py
@@ -1,3 +1,5 @@
+import functools
+
 import jax
 import jax.numpy as jnp
 from jax import lax
@@ -11,7 +13,7 @@
 SX, SY, SZ = 4, 128, 128
 CY = 32
 PAD = 8
-PIECES = ((0, 8), (120, 8), (8, 32), (40, 32), (72, 48))
+PIECES = ((0, 8), (120, 8), (8, 16), (24, 32), (56, 32), (88, 32))
 EDGES = 2
 PHASE, SOLUTE = 0, 1
 
@@ -196,23 +198,38 @@
     def first_phase(x, c):
         rows = pl.ds(PAD + PIECES[c][0], PIECES[c][1])
         p, near = neighbours(0, x, PHASE, c)
-        w[1, x + 1, PHASE, rows, :] = next_phase(p, near, w[1, x + 1, SOLUTE, rows, :], c)
+        new = next_phase(p, near, w[1, x + 1, SOLUTE, rows, :], c)
+
+        def store():
+            w[1, x + 1, PHASE, rows, :] = new
+
+        return store
 
     def fused(x, c, a, b):
         rows = pl.ds(PAD + PIECES[c][0], PIECES[c][1])
         p, near = neighbours(a, x, PHASE, c)
         u, unear = neighbours(a, x, SOLUTE, c)
         u = next_solute(p, near, u, unear, w[b, x + 1, PHASE, rows, :])
-        w[b, x + 1, SOLUTE, rows, :] = u
-        w[b, x + 1, PHASE, rows, :] = next_phase(p, near, u, c)
+        new = next_phase(p, near, u, c)
+
+        def store():
+            w[b, x + 1, SOLUTE, rows, :] = u
+            w[b, x + 1, PHASE, rows, :] = new
+
+        return store
 
     def last_solute(x, c):
         rows = pl.ds(PAD + PIECES[c][0], PIECES[c][1])
         p, near = neighbours(0, x, PHASE, c)
         u, unear = neighbours(0, x, SOLUTE, c)
         out = pl.ds(*PIECES[c])
-        solute_out[x, out, :] = next_solute(p, near, u, unear, w[1, x + 1, PHASE, rows, :])
-        phase_out[x, out, :] = p
+        new = next_solute(p, near, u, unear, w[1, x + 1, PHASE, rows, :])
+
+        def store():
+            solute_out[x, out, :] = new
+            phase_out[x, out, :] = p
+
+        return store
 
     zi = lax.broadcasted_iota(jnp.int32, (128, 128), 0)
     zj = lax.broadcasted_iota(jnp.int32, (128, 128), 1)
@@ -251,19 +268,29 @@
     def layers(step, slot_in, slot_out, send, fields):
         taken = (PHASE, SOLUTE) if fields.size == 2 else (PHASE,)
         take_edges(slot_in, taken)
-        for c in range(len(PIECES)):
-            if c == EDGES:
-                take_z(slot_in)
+        for store in [step(x, c) for c in range(EDGES) for x in (1, 2)]:
+            store()
+        for c in range(EDGES):
+            for side in range(2):
+                x_copy(slot_in, side, c, fields).wait_recv()
+        for store in [step(x, c) for c in range(EDGES) for x in (0, 3)]:
+            store()
+        if send:
+            for c in range(EDGES):
+                for side in range(2):
+                    x_copy(slot_out, side, c).start()
+        if send:
+            send_y(slot_out)
+            send_edge_z(slot_out)
+        take_z(slot_in)
+        for c in range(EDGES, len(PIECES)):
             for x in (1, 2):
-                step(x, c)
+                step(x, c)()
             for x, side in ((0, 0), (3, 1)):
                 x_copy(slot_in, 1 - side, c, fields).wait_recv()
-                step(x, c)
+                step(x, c)()
                 if send:
                     x_copy(slot_out, side, c).start()
-            if send and c == EDGES - 1:
-                send_y(slot_out)
-                send_edge_z(slot_out)
         if send:
             send_z(slot_out)
         for c in range(len(PIECES)):
@@ -294,26 +321,17 @@
         t_copy(1, k).start()
     set_fine()
 
-    def substep(r, carry):
-        b = lax.rem(r, 2)
-        a = 1 - b
-        layers(lambda x, c: fused(x, c, a, b), a, b, True, pl.ds(0, 2))
+    for r in (2, 3, 4):
+        a, b = 1 - r % 2, r % 2
+        layers(functools.partial(fused, a=a, b=b), a, b, True, pl.ds(0, 2))
         next_temp(a, b)
-
-        @pl.when(r < 4)
-        def _():
+        if r < 4:
             for k in range(6):
                 t_copy(b, k).start()
-
-        @pl.when(r == 4)
-        def _():
+            set_fine()
+        else:
             for k in range(1, NGX):
                 g_copy(k).start()
-
-        set_fine()
-        return carry
-
-    lax.fori_loop(2, 5, substep, 0)
 
     layers(last_solute, 0, None, False, pl.ds(0, 2))
     for k in range(1, NGX):

time: 41 us -> 40.4 us (0.985)
  Pallas kernels: 40.2 us -> 39.7 us
    pallas_call x1, Pallas kernels: 39.3 us -> 38.7 us  [per_device(): pl.pallas_call(kernel, out_shape=(block, block, jax.ShapeDtypeStruct((CY,...]
where the time goes in v4:
time: 40.4 us; the launch traced here: 40.3 us
  Pallas kernels  39.7 us (98%)
  between operations  0.64 us (2%)
    pallas_call x1, Pallas kernels, per_device(): pl.pallas_call(kernel, out_shape=(block, block, jax.ShapeDtypeStruct((CY,...  38.7 us
    pallas_call x1, Pallas kernels, per_device(): pl.pallas_call(finish, out_shape=(block, block, jax.ShapeDtypeStruct((CY,...  0.9 us

profile of v4, /device:TPU:1, one launch (start us, length us, event | category | flops | bytes accessed | tf_op | source)
XLA Modules:
  0.0 40.3 jit_solution(17748211550978745715)
XLA Ops:
  0.6 38.7 %solidify.1 = (f32[4,128,128]{2,1,0:T(8,128)S(1)}, f32[4,128,128]{2,1,0:T(8,128)S(1)}, f32[32,16,32]{2,1,0:T(8,128)S(1)}) custom-call(f32[4,128,128]{2,1,0:T(8,128)} %phase_in.1, f32[4,128,128]{2,1,0:T(8,128)} %solute_in.1, f32[32,16,32]{2,1,0:T(8,128)} %bitcast.2), custom_call_target="tpu_custom_call" | custom-call | tf_op jit(solution)/shard_map/solidify/pallas_call | solution.py:363
  39.4 0.9 %finish.1 = (f32[4,128,128]{2,1,0:T(8,128)}, f32[4,128,128]{2,1,0:T(8,128)}, f32[32,16,32]{2,1,0:T(8,128)}) custom-call(f32[4,128,128]{2,1,0:T(8,128)S(1)} %get-tuple-element.9.phase, f32[4,128,128]{2,1,0:T(8,128)S(1)} %get-tuple-element.10.solute, f32[32,16,32]{2,1,0:T(8,128)S(1)} %get-tuple-element.11.temp), custom_call_target="tpu_custom_call" | custom-call | tf_op jit(solution)/shard_map/finish/pallas_call | solution.py:397
